TPU v7x, 32 devices: a whole 2x2x4 slice. The times are simulated.
32 devices in a mesh: ctx: 8 (over z, y), fsdp: 4 (over x, core).
Axes of the slice: x: 2, y: 2, z: 4, core: 2. Of those that a mesh axis runs over, the one named last changes fastest.
Arguments:
- inputs: bfloat16 [4, 4096, 2048], P('fsdp', 'ctx'), may hold values from -6 to 6
- queries: bfloat16 [4, 4096, 512], P('fsdp', 'ctx'), may hold values from -5 to 5
- key_vectors: bfloat16 [4, 4096, 128], P('fsdp', 'ctx'), may hold values from -5 to 5
- w_value: bfloat16 [2048, 128], P('fsdp'), may hold values from -0.125 to 0.125
- grad_out: bfloat16 [4, 4096, 512], P('fsdp', 'ctx'), may hold values from -6 to 6
- block_picks: int32 [4, 8, 2], P('fsdp'), may hold values from 0 to 6, as said below
Outputs:
- grad_queries: bfloat16 [4, 4096, 512], P('fsdp', 'ctx')
- grad_keys: bfloat16 [4, 4096, 128], P('fsdp', 'ctx')
- grad_values: bfloat16 [4, 4096, 128], P('fsdp', 'ctx')
- grad_weight: bfloat16 [2048, 128], P(('ctx', 'fsdp'))
Inputs may be any that keep to these rules, and one draw needn't show every extreme that they name: `block_picks`: for query block b of a sequence the two entries are block indices no greater than b: for b >= 2 two different blocks below b, for b = 1 the pair 0 and 1, for b = 0 both 0. The last query block of every sequence selects block 6 as its second entry.
All inputs are finite; a program needn't handle non-finite values.
Results may differ from a plain program's by a relative error of at most 0.015.
Values may be sent and summed in bfloat16 or wider, within the bound.
A program may use at most 64 MiB of HBM per device.

v0:
```python
import math

import jax
import jax.numpy as jnp
from jax import lax
from jax.sharding import PartitionSpec as P

HEAD = 128
GROUP = 4
BLOCK = 512


NEG = -1e30


def on_device(inputs, queries, key_vectors, w_value, grad_out, block_picks):
    row_count = inputs.shape[1]
    ctx_count = lax.axis_size("ctx")
    my_place = lax.axis_index("ctx")
    source = inputs[0]
    inv_root = 1.0 / math.sqrt(HEAD)
    local_count = row_count // BLOCK
    block_count = row_count * ctx_count // BLOCK
    columns = source
    projected = jnp.dot(
        columns,
        lax.all_gather(w_value, "fsdp", axis=0, tiled=True),
        preferred_element_type=jnp.float32,
    ).astype(jnp.bfloat16)
    paired = jnp.concatenate([key_vectors[0], projected], axis=1)
    pick_table = block_picks[0]
    own_ids = my_place * local_count + jnp.arange(local_count, dtype=jnp.int32)
    own_picks = lax.dynamic_slice_in_dim(pick_table, my_place * local_count, local_count, 0)
    picks_flat = own_picks.reshape(-1)
    pick_rows = jnp.repeat(picks_flat, BLOCK) * BLOCK + jnp.tile(
        jnp.arange(BLOCK, dtype=jnp.int32), 2 * local_count
    )
    kv_piece = lax.all_gather(paired, "ctx", axis=0, tiled=True)
    piece_rows = kv_piece.shape[0]
    inside_piece = (pick_rows >= 0) & (pick_rows < piece_rows)
    picked_rows = jnp.take(kv_piece, jnp.clip(pick_rows, 0, piece_rows - 1), axis=0)
    fetched = jnp.where(
        inside_piece[:, None],
        picked_rows,
        jnp.zeros((2 * local_count * BLOCK, 2 * HEAD), jnp.bfloat16),
    )
    slot_of = jnp.repeat(jnp.arange(3, dtype=jnp.int32), BLOCK)
    block_id = own_ids[0]
    chosen = jnp.concatenate([block_id[None], own_picks[0]])
    kv_block = jnp.concatenate([paired, fetched], axis=0)
    key_block = kv_block[:, :HEAD]
    value_block = kv_block[:, HEAD:]
    query_rows = queries[0, 0:BLOCK].reshape(BLOCK, GROUP, HEAD).transpose(1, 0, 2)
    grad_rows = grad_out[0, 0:BLOCK].reshape(BLOCK, GROUP, HEAD).transpose(1, 0, 2)
    query_pos = block_id * BLOCK + jnp.arange(BLOCK, dtype=jnp.int32)
    key_pos = (chosen[:, None] * BLOCK + jnp.arange(BLOCK, dtype=jnp.int32)[None, :]).reshape(-1)
    usable = chosen != block_id
    allowed = jnp.where(
        slot_of[None, :] == 0, key_pos[None, :] <= query_pos[:, None], usable[slot_of][None, :]
    )

    def head_pass(totals, head_items):
        query_head, grad_head = head_items
        scores = (
            jnp.einsum("th,uh->tu", query_head, key_block, preferred_element_type=jnp.float32)
            * inv_root
        )
        masked = jnp.where(allowed, scores, NEG)
        highest = jnp.max(masked, axis=1, keepdims=True)
        exp_terms = jnp.where(allowed, jnp.exp(masked - highest), 0.0)
        weights = exp_terms / jnp.sum(exp_terms, axis=1, keepdims=True)
        weights_low = weights.astype(jnp.bfloat16)
        attended = jnp.dot(weights_low, value_block, preferred_element_type=jnp.float32)
        row_delta = jnp.sum(grad_head.astype(jnp.float32) * attended, axis=1)
        dweights = jnp.einsum(
            "th,uh->tu", grad_head, value_block, preferred_element_type=jnp.float32
        )
        dscores = (weights * (dweights - row_delta[:, None])).astype(jnp.bfloat16)
        grad_query_head = (
            jnp.dot(dscores, key_block, preferred_element_type=jnp.float32) * inv_root
        ).astype(jnp.bfloat16)
        key_total = totals[0] + jnp.einsum(
            "tu,th->uh", dscores, query_head, preferred_element_type=jnp.float32
        )
        value_total = totals[1] + jnp.einsum(
            "tu,th->uh", weights_low, grad_head, preferred_element_type=jnp.float32
        )
        return ((key_total, value_total), grad_query_head)

    empty = jnp.zeros((3 * BLOCK, HEAD), jnp.float32)
    totals, grad_heads_out = lax.scan(head_pass, (empty, empty), (query_rows, grad_rows))
    grad_list = grad_heads_out.transpose(1, 0, 2).reshape(BLOCK, GROUP * HEAD)
    partial_list = jnp.concatenate([totals[0] * inv_root, totals[1]], axis=1).reshape(
        3, BLOCK, 2 * HEAD
    )
    flat_ids = jnp.concatenate([own_ids[:, None], own_picks], axis=1).reshape(-1)
    same_block = (flat_ids[:, None] == flat_ids[None, :]).astype(jnp.float32)
    combined = jnp.einsum("jk,krc->jrc", same_block, partial_list, precision=lax.Precision.HIGHEST)
    spread = (
        jnp.zeros((block_count, BLOCK, 2 * HEAD), jnp.bfloat16)
        .at[flat_ids]
        .set(combined.astype(jnp.bfloat16))
    )
    arrived = lax.all_to_all(spread, "ctx", split_axis=0, concat_axis=0, tiled=True)
    summed = jnp.sum(arrived, axis=0, dtype=jnp.float32)
    grad_key_rows = summed[:, :HEAD].astype(jnp.bfloat16)
    grad_value_rows = summed[:, HEAD:].astype(jnp.bfloat16)
    columns = source
    middle_sum = lax.psum_scatter(
        jnp.einsum(
            "tc,th->ch", columns, grad_value_rows, preferred_element_type=jnp.float32
        ).astype(jnp.bfloat16),
        "ctx",
        scatter_dimension=0,
        tiled=True,
    )
    grad_weight = lax.psum_scatter(middle_sum, "fsdp", scatter_dimension=0, tiled=True).astype(
        jnp.float32
    )
    return (
        grad_list.reshape(1, row_count, GROUP * HEAD),
        grad_key_rows[None],
        grad_value_rows[None],
        grad_weight.astype(jnp.bfloat16),
    )


def solution(mesh):
    in_specs = (
        P("fsdp", "ctx", None),
        P("fsdp", "ctx", None),
        P("fsdp", "ctx", None),
        P("fsdp", None),
        P("fsdp", "ctx", None),
        P("fsdp", None, None),
    )
    out_specs = (
        P("fsdp", "ctx", None),
        P("fsdp", "ctx", None),
        P("fsdp", "ctx", None),
        P(("ctx", "fsdp"), None),
    )
    return jax.shard_map(
        on_device, mesh=mesh, in_specs=in_specs, out_specs=out_specs, check_vma=False
    )
```

profile of v0, /device:TPU:0, one launch (start us, length us, event | category | flops | bytes accessed | tf_op | source)
XLA Modules:
  0.0 300.3 jit_solution(15653211364276626113)
XLA Ops:
  7.2 9.0 %all_gather.6 = bf16[2048,128]{1,0:T(8,128)(2,1)S(1)} all-gather(bf16[512,128]{1,0:T(8,128)(2,1)} %param.11), channel_id=1, replica_groups=mesh['ctx'=8,'fsdp'=4] {'fsdp'}, dimensions={0}, use_global_device_ids=true | all-gather | bytes 655360 | tf_op jit(solution)/shard_map/all_gather | solution.py:27
  27.2 43.8 %all-gather.2.cloned.1.call-done = bf16[4096,256]{0,1:T(8,128)(2,1)} async-done(((bf16[512,256]{0,1:T(8,128)(2,1)}), bf16[4096,256]{0,1:T(8,128)(2,1)}) %all-gather.2.cloned.1.call-update) | async-done | bytes 2097168 | tf_op jit(solution)/shard_map/all_gather | solution.py:38
  70.9 4.1 %copy.28 = bf16[4096,256]{1,0:T(8,128)(2,1)} copy(bf16[4096,256]{0,1:T(8,128)(2,1)} %all-gather.2.cloned.1.call-done) | data formatting | bytes 4194304 | tf_op jit(solution)/shard_map/all_gather | solution.py:38
  75.0 5.3 %gather_fusion = bf16[1024,256]{1,0:T(8,128)(2,1)S(1)} fusion(bf16[4096,256]{1,0:T(8,128)(2,1)} %copy.28, s32[1024]{0:T(1024)S(1)} %broadcast_clamp_fusion), kind=kCustom, calls=%fused_computation | custom fusion | bytes 1052672 | tf_op jit(solution)/shard_map/jit(_take)/gather | solution.py:41
  82.5 63.9 %while.15 = (s32[]{:T(128)}, f32[1536,128]{1,0:T(8,128)S(1)}, f32[1536,128]{1,0:T(8,128)}, bf16[4,512,128]{2,1,0:T(8,128)(2,1)}, bf16[4,512,128]{1,2,0:T(8,128)(...) while((s32[]{:T(128)}, f32[1536,128]{1,0:T(8,128)S(1)}, ...), condition=%wide.region_4.5_spmd.clone, body=%wide.region_0.4_spmd.clone.sunk | while | flops 1224800768 | bytes 59557096 | solution.py:91
  82.5 2.2 fusion.85
  90.6 2.5 convolution_add_fusion.4
  93.1 2.7 fusion.90
  95.8 2.4 convolution_add_fusion.5
  98.2 2.2 fusion.85
  106.3 2.5 convolution_add_fusion.4
  108.8 2.7 fusion.90
  111.5 2.7 convolution_add_fusion.5
  122.4 2.5 convolution_add_fusion.4
  124.9 2.7 fusion.90
  127.6 2.7 convolution_add_fusion.5
  138.4 2.5 convolution_add_fusion.4
  140.9 2.7 fusion.90
  143.6 2.7 convolution_add_fusion.5
  147.7 2.9 fusion.31
  152.2 2.6 scatter_fusion
  154.9 52.4 %all_to_all.5 = bf16[8,512,256]{2,1,0:T(8,128)(2,1)} all-to-all(bf16[8,512,256]{2,1,0:T(8,128)(2,1)} %scatter_fusion), channel_id=1, replica_groups=mesh['ctx'=8,'fsdp'=4] {'ctx'}, dimensions={0} | all-to-all | bytes 4194304 | tf_op jit(solution)/shard_map/all_to_all | solution.py:104
  212.0 60.2 %reduce-scatter.5.cloned.1.call-done = bf16[256,128]{0,1:T(8,128)(2,1)} async-done(((bf16[2048,128]{0,1:T(8,128)(2,1)}), bf16[256,128]{0,1:T(8,128)(2,1)}) %reduce-scatter.5.cloned.1.call-update) | async-done | bytes 65552 | tf_op jit(solution)/shard_map/reduce_scatter | solution.py:109
  274.5 19.3 %reduce-scatter.7.cloned.1.call-done = bf16[64,128]{1,0:T(8,128)(2,1)} async-done(((bf16[256,128]{1,0:T(8,128)(2,1)}), bf16[64,128]{1,0:T(8,128)(2,1)}) %reduce-scatter.7.cloned.1.call-update) | async-done | bytes 16400
  (100 shorter events, 50.9 us)
Async XLA Ops:
  7.2 10.1 %copy-start = (bf16[1,512,2048]{2,1,0:T(8,128)(2,1)S(1)}, bf16[1,512,2048]{2,1,0:T(8,128)(2,1)}, u32[]{:S(2)}) copy-start(bf16[1,512,2048]{2,1,0:T(8,128)(2,1)} %param.8) | copy-start | bytes 6291460
  7.2 13.5 %copy-start.6 = (s32[1,8,2]{1,2,0:T(2,128)S(1)}, s32[1,8,2]{1,2,0:T(2,128)}, u32[]{:S(2)}) copy-start(s32[1,8,2]{1,2,0:T(2,128)} %param.13) | copy-start | bytes 196
  7.2 14.0 %copy-start.4 = (bf16[1,512,512]{2,1,0:T(8,128)(2,1)S(1)}, bf16[1,512,512]{2,1,0:T(8,128)(2,1)}, u32[]{:S(2)}) copy-start(bf16[1,512,512]{2,1,0:T(8,128)(2,1)} %param.9) | copy-start | bytes 1572868
  7.2 63.7 %all-gather.2.cloned.1.call-start = ((), (), s32[]{:S(2)}) async-start(), calls=%async_computation.3 | async-start | bytes 2359296 | tf_op jit(solution)/shard_map/all_gather | solution.py:38
  18.8 253.4 %reduce-scatter.5.cloned.1.call-start = ((), (), s32[]{:S(2)}) async-start(), calls=%async_computation.4 | async-start | bytes 589824 | tf_op jit(solution)/shard_map/reduce_scatter | solution.py:109
  85.8 1.3 copy-start.3
  87.1 1.7 copy-start.1
  90.6 5.2 %copy-start.2 = (f32[512,1536]{1,0:T(8,128)S(1)}, f32[512,1536]{1,0:T(8,128)}, u32[]{:S(2)}) copy-start(f32[512,1536]{1,0:T(8,128)} %copy-done.1) | copy-start | bytes 9437188 | tf_op jit(solution)/shard_map/while
  101.5 1.3 copy-start.3
  102.8 1.7 copy-start.1
  106.3 5.2 %copy-start.2 = (f32[512,1536]{1,0:T(8,128)S(1)}, f32[512,1536]{1,0:T(8,128)}, u32[]{:S(2)}) copy-start(f32[512,1536]{1,0:T(8,128)} %copy-done.1) | copy-start | bytes 9437188 | tf_op jit(solution)/shard_map/while
  117.6 1.3 copy-start.3
  118.8 1.7 copy-start.1
  122.4 5.2 %copy-start.2 = (f32[512,1536]{1,0:T(8,128)S(1)}, f32[512,1536]{1,0:T(8,128)}, u32[]{:S(2)}) copy-start(f32[512,1536]{1,0:T(8,128)} %copy-done.1) | copy-start | bytes 9437188 | tf_op jit(solution)/shard_map/while
  133.6 1.3 copy-start.3
  134.9 1.7 copy-start.1
  138.4 5.2 %copy-start.2 = (f32[512,1536]{1,0:T(8,128)S(1)}, f32[512,1536]{1,0:T(8,128)}, u32[]{:S(2)}) copy-start(f32[512,1536]{1,0:T(8,128)} %copy-done.1) | copy-start | bytes 9437188 | tf_op jit(solution)/shard_map/while
  207.2 3.4 %copy-start.5 = (bf16[4,512,128]{2,1,0:T(8,128)(2,1)S(1)}, bf16[4,512,128]{2,1,0:T(8,128)(2,1)}, u32[]{:S(2)}) copy-start(bf16[4,512,128]{2,1,0:T(8,128)(2,1)} %get-tuple-element.53) | copy-start | bytes 1572868
  210.5 83.3 %reduce-scatter.7.cloned.1.call-start = ((), (), s32[]{:S(2)}) async-start(), calls=%async_computation.5 | async-start | bytes 81920
Sparse Core Ops, SparseCore 0:
  18.9 51.9 all-gather.1
  210.7 61.5 reduce-scatter.4
  275.3 18.4 reduce-scatter.6
where the time goes:
time: 301 us; the launch traced here: 300 us
  waiting for transfers between devices  123 us (41%)
  blocking collectives  61.3 us (20%)
  matrix products  55.4 us (18%)
  local copies, waits for them, and re-layouts  28 us (9%)
  other arithmetic  18.2 us (6%)
  between operations  13.9 us (5%)
    reduce_scatter x1, waiting for transfers between devices, on_device(): lax.psum_scatter(jnp.einsum('tc,th->ch', columns, grad_value_rows, prefer...  60.2 us
    all_to_all x1, blocking collectives, on_device(): lax.all_to_all(spread, 'ctx', split_axis=0, concat_axis=0, tiled=True)  52.4 us
    all_gather x1, waiting for transfers between devices, on_device(): kv_piece = lax.all_gather(paired, 'ctx', axis=0, tiled=True)  43.8 us
    unnamed x4, waiting for transfers between devices  19.3 us
    dot_general x4, matrix products, head_pass(): jnp.dot(dscores, key_block, preferred_element_type=jnp.float32) * inv_root  10.8 us
    dot_general x4, matrix products, head_pass(): jnp.einsum('tu,th->uh', weights_low, grad_head, preferred_element_type=jn...  10.6 us
    dot_general x4, matrix products, head_pass(): jnp.einsum('tu,th->uh', dscores, query_head, preferred_element_type=jnp.f...  9.97 us
    all_gather x1, blocking collectives, on_device(): lax.all_gather(w_value, 'fsdp', axis=0, tiled=True)  8.96 us
  transfers between devices with their start and end apart: 3, of which 3 were waited for; matrix products, arithmetic and copies ran while one was open for 3% of the time, Pallas kernels for 0%

commit v1 on v0

v1 whole, which is shorter than its diff:
```python
import math

import jax
import jax.numpy as jnp
from jax import lax
from jax.experimental import pallas as pl
from jax.experimental.pallas import tpu as pltpu
from jax.sharding import PartitionSpec as P

HEAD = 128
GROUP = 4
BLOCK = 512
NEG = -1e30
MESH = pl.DeviceIdType.MESH
F32 = jnp.float32
BF16 = jnp.bfloat16
VM = pltpu.VMEM


def bits_of(count):
    bits, bit = [], 1
    while bit < count:
        bits.append(bit)
        bit *= 2
    return bits


def remote(src, dst, send, recv, **where):
    return pltpu.make_async_remote_copy(
        src_ref=src,
        dst_ref=dst,
        send_sem=send,
        recv_sem=recv,
        device_id=where,
        device_id_type=MESH,
    )


def greet(n, nf, direct):
    c, f = lax.axis_index("ctx"), lax.axis_index("fsdp")
    lines = n // 2
    y, z = c % 2, c // 2
    barrier = pltpu.get_barrier_semaphore()
    count = 0
    for bit in bits_of(nf):
        mine = (f // bit) % 2
        pl.semaphore_signal(
            barrier, inc=1, device_id={"fsdp": f + bit - 2 * bit * mine}, device_id_type=MESH
        )
        count += 1
    pl.semaphore_signal(
        barrier, inc=1, device_id={"ctx": 2 * z + (1 - y)}, device_id_type=MESH
    )
    count += 1
    if direct:
        for o in range(1, lines):
            pl.semaphore_signal(
                barrier, inc=1, device_id={"ctx": 2 * ((z + o) % lines) + y}, device_id_type=MESH
            )
            count += 1
        pl.semaphore_wait(barrier, count)
    else:
        pl.semaphore_wait(barrier, count)

        @pl.when(z > 0)
        def _():
            pl.semaphore_signal(barrier, inc=1, device_id={"ctx": c - 2}, device_id_type=MESH)

        @pl.when(z < lines - 1)
        def _():
            pl.semaphore_signal(barrier, inc=1, device_id={"ctx": c + 2}, device_id_type=MESH)

        @pl.when(z > 0)
        def _():
            pl.semaphore_wait(barrier, 1)

        @pl.when(z < lines - 1)
        def _():
            pl.semaphore_wait(barrier, 1)


def gather_kernel(
    n, nf, x_ref, k_ref, w_ref, kall, vall, wbuf, w_send, w_recv,
    kz_send, vz_send, ky_send, vy_send, k_recv, v_recv,
):
    c, f = lax.axis_index("ctx"), lax.axis_index("fsdp")
    lines = n // 2
    y, z = c % 2, c // 2
    partner = 2 * z + (1 - y)
    ws = w_ref.shape[0]
    wbuf[f] = w_ref[...]
    kall[c] = k_ref[...]
    greet(n, nf, True)

    def up(buf, b, send, recv):
        return remote(buf.at[b], buf.at[b], send.at[b], recv.at[b], ctx=c + 2)

    def across(buf, b, send, recv):
        return remote(buf.at[b], buf.at[b], send.at[b], recv.at[b], ctx=partner)

    held = [f]
    bits = bits_of(nf)
    slot = 0
    stages = []
    for bit in reversed(bits):
        mine = (f // bit) % 2
        other = bit - 2 * bit * mine
        stages.append((bit, other))

    def w_stage(index, held, slot):
        bit, other = stages[index]
        copies = []
        for g in held:
            copies.append(
                remote(wbuf.at[g], wbuf.at[g], w_send.at[slot], w_recv.at[slot], fsdp=f + other)
            )
            slot += 1
        for copy in copies:
            copy.start()
        return copies, [g + other for g in held], slot

    def forward(buf, b, zsend, ysend, recv, first):
        @pl.when(z < lines - 1)
        def _():
            up(buf, b, zsend, recv).start()

        if first:
            @pl.when(y == 0)
            def _():
                across(buf, b, ysend, recv).start()
        else:
            across(buf, b, ysend, recv).start()

    total = None

    def add(total, g):
        columns = pl.ds(pl.multiple_of(g * ws, ws), ws)
        term = jnp.dot(x_ref[:, columns], wbuf[g], preferred_element_type=F32)
        return term if total is None else total + term

    for index in range(len(stages)):
        copies, came, slot = w_stage(index, held, slot)
        if index == 0:
            forward(kall, c, kz_send, ky_send, k_recv, True)
            total = add(total, f)
        for copy in copies:
            copy.wait()
        held = held + came
    for g in held[1:]:
        total = add(total, g)
    vall[c] = total.astype(BF16)
    forward(vall, c, vz_send, vy_send, v_recv, True)

    for s in range(1, lines):
        b = c - 2 * s

        @pl.when(z - s >= 0)
        def _():
            up(kall, b, kz_send, k_recv).wait_recv()
            forward(kall, b, kz_send, ky_send, k_recv, False)
            up(vall, b, vz_send, v_recv).wait_recv()
            forward(vall, b, vz_send, vy_send, v_recv, False)

    @pl.when(y == 1)
    def _():
        across(kall, partner, ky_send, k_recv).wait_recv()
        across(vall, partner, vy_send, v_recv).wait_recv()

    for s in range(1, lines):
        @pl.when(z - s >= 0)
        def _():
            across(kall, partner - 2 * s, ky_send, k_recv).wait_recv()
            across(vall, partner - 2 * s, vy_send, v_recv).wait_recv()

    for s in range(lines):
        b = c - 2 * s

        @pl.when(z - s >= 0)
        def _():
            @pl.when(z < lines - 1)
            def _():
                up(kall, b, kz_send, k_recv).wait_send()
                up(vall, b, vz_send, v_recv).wait_send()

            def done():
                across(kall, b, ky_send, k_recv).wait_send()
                across(vall, b, vy_send, v_recv).wait_send()

            if s == 0:
                pl.when(y == 0)(done)
            else:
                done()


def attend_kernel(
    ids, q_ref, g_ref, k0, k1, k2, v0, v1, v2, dq_ref, own_k, own_v, slot_k, slot_v, dk_acc, dv_acc
):
    h = pl.program_id(0)
    inv_root = 1.0 / math.sqrt(HEAD)
    q = q_ref[...]
    g = g_ref[...]
    ks = [k0[...], k1[0], k2[0]]
    vs = [v0[0], v1[0], v2[0]]
    nt = (((1,), (1,)), ((), ()))
    tn = (((0,), (0,)), ((), ()))
    scores = []
    for j in range(3):
        s = lax.dot_general(ks[j], q, nt, preferred_element_type=F32) * inv_root
        if j == 0:
            u = lax.broadcasted_iota(jnp.int32, s.shape, 0)
            t = lax.broadcasted_iota(jnp.int32, s.shape, 1)
            s = jnp.where(u <= t, s, NEG)
        else:
            s = jnp.where(ids[j] != ids[0], s, NEG)
        scores.append(s)
    highest = jnp.max(
        jnp.maximum(jnp.maximum(scores[0], scores[1]), scores[2]), axis=0, keepdims=True
    )
    exps = [jnp.exp(s - highest) for s in scores]
    norm = 1.0 / jnp.sum(exps[0] + exps[1] + exps[2], axis=0, keepdims=True)
    weights = [e * norm for e in exps]
    lows = [w.astype(BF16) for w in weights]
    dws = [lax.dot_general(v, g, nt, preferred_element_type=F32) for v in vs]
    delta = jnp.sum(
        sum(low.astype(F32) * dw for low, dw in zip(lows, dws)), axis=0, keepdims=True
    )
    ds = [(w * (dw - delta)).astype(BF16) for w, dw in zip(weights, dws)]
    dq = sum(lax.dot_general(d, k, tn, preferred_element_type=F32) for d, k in zip(ds, ks))
    dq_ref[...] = (dq * inv_root).astype(BF16)

    @pl.when(h == 0)
    def _():
        dk_acc[...] = jnp.zeros_like(dk_acc)
        dv_acc[...] = jnp.zeros_like(dv_acc)

    for j in range(3):
        dk_acc[j] += jnp.dot(ds[j], q, preferred_element_type=F32)
        dv_acc[j] += jnp.dot(lows[j], g, preferred_element_type=F32)

    @pl.when(h == GROUP - 1)
    def _():
        own_k[...] = dk_acc[0] * inv_root
        own_v[...] = dv_acc[0]
        for j in (1, 2):
            slot_k[j - 1] = (dk_acc[j] * inv_root).astype(BF16)
            slot_v[j - 1] = dv_acc[j].astype(BF16)


def reduce_kernel(
    n, nf, picks, x_ref, own_k, own_v, slot_k, slot_v, gk_ref, gv_ref, gw_ref,
    pslot_k, pslot_v, sbuf_k, sbuf_v, rbuf_k, rbuf_v, acc, wsend, wrecv, ysend_buf, yrecv_buf,
    zsend_buf, zrecv_buf, p_send, p_recv, c_send, c_recv, f_send, f_recv, y_sem, z_send, z_recv,
):
    c, f = lax.axis_index("ctx"), lax.axis_index("fsdp")
    lines = n // 2
    y, z = c % 2, c // 2
    partner = 2 * z + (1 - y)
    greet(n, nf, True)
    sides = []
    for side, (slots, pslots) in enumerate(((slot_v, pslot_v), (slot_k, pslot_k))):
        copy = remote(slots, pslots, p_send.at[side], p_recv.at[side], ctx=partner)
        copy.start()
        sides.append(copy)

    def chain(side):
        own, slots, pslots, sbuf, rbuf, out = (
            (own_v, slot_v, pslot_v, sbuf_v, rbuf_v, gv_ref),
            (own_k, slot_k, pslot_k, sbuf_k, rbuf_k, gk_ref),
        )[side]

        def down(zd):
            return remote(
                sbuf.at[zd], rbuf.at[zd], c_send.at[side, zd], c_recv.at[side, zd], ctx=c - 2
            )

        sides[side].wait()
        for zd in range(lines):
            @pl.when(zd <= z)
            def _():
                dest = 2 * zd + y
                value = jnp.zeros(own.shape, F32)
                for owner, held in ((c, slots), (partner, pslots)):
                    for j in range(2):
                        gate = jnp.where(picks[owner, j] == dest, 1.0, 0.0).astype(F32)
                        value = value + held[j].astype(F32) * gate
                sbuf[zd] = value.astype(BF16)

                @pl.when(z < lines - 1)
                def _():
                    down(zd).wait_recv()
                    sbuf[zd] = (value + rbuf[zd].astype(F32)).astype(BF16)

                @pl.when(zd < z)
                def _():
                    down(zd).start()

                @pl.when(zd == z)
                def _():
                    out[...] = (sbuf[zd].astype(F32) + own[...]).astype(BF16)

        return down

    down_v = chain(0)
    gv = gv_ref[...]
    rows = x_ref.shape[1] // (n * nf)
    group = x_ref.shape[1] // n
    tn = (((0,), (0,)), ((), ()))
    part = lax.dot_general(x_ref[...], gv, tn, preferred_element_type=F32)
    for cc in range(n):
        for ff in range(nf):
            at = cc * group + ff * rows
            acc[ff, cc] = part[at : at + rows]

    slot = 0
    copies = []
    for stage, bit in enumerate(bits_of(nf)):
        mine = (f // bit) % 2
        low = f % bit
        now = []
        for hi in range(nf // (2 * bit)):
            away = hi * 2 * bit + (1 - mine) * bit + low
            wsend[slot] = acc[away].astype(BF16)
            copy = remote(
                wsend.at[slot], wrecv.at[slot], f_send.at[slot], f_recv.at[slot],
                fsdp=f + bit - 2 * bit * mine,
            )
            copy.start()
            now.append((copy, hi * 2 * bit + mine * bit + low, slot))
            slot += 1
        for copy, keep, at in now:
            copy.wait()
            acc[keep] += wrecv[at].astype(F32)
    for zz in range(lines):
        ysend_buf[zz] = acc[f, 2 * zz + (1 - y)].astype(BF16)
    copy = remote(ysend_buf, yrecv_buf, y_sem.at[0], y_sem.at[1], ctx=partner)
    copy.start()
    copy.wait()
    now = []
    for o in range(1, lines):
        zz = (z + o) % lines
        zsend_buf[o] = (acc[f, 2 * zz + y] + yrecv_buf[zz].astype(F32)).astype(BF16)
        copy = remote(
            zsend_buf.at[o], zrecv_buf.at[o], z_send.at[o], z_recv.at[o], ctx=2 * zz + y
        )
        copy.start()
        now.append(copy)
    total = acc[f, c] + yrecv_buf[z].astype(F32)
    for o, copy in enumerate(now):
        copy.wait()
        total = total + zrecv_buf[o + 1].astype(F32)
    gw_ref[...] = total.astype(BF16)

    down_k = chain(1)
    for zd in range(lines):
        @pl.when(zd < z)
        def _():
            down_v(zd).wait_send()
            down_k(zd).wait_send()


def on_device(inputs, queries, key_vectors, w_value, grad_out, block_picks):
    n, nf = lax.axis_size("ctx"), lax.axis_size("fsdp")
    c = lax.axis_index("ctx")
    lines = n // 2
    x, q, k, g, picks = inputs[0], queries[0], key_vectors[0], grad_out[0], block_picks[0]
    dma = pltpu.SemaphoreType.DMA
    vmem = pl.BlockSpec(memory_space=VM)
    smem = pl.BlockSpec(memory_space=pltpu.SMEM)
    ws = w_value.shape[0]
    kall, vall = pl.pallas_call(
        lambda *refs: gather_kernel(n, nf, *refs),
        out_shape=[jax.ShapeDtypeStruct((n, BLOCK, HEAD), BF16)] * 2,
        in_specs=[vmem] * 3,
        out_specs=[vmem] * 2,
        scratch_shapes=[VM((nf, ws, HEAD), BF16), dma((nf,)), dma((nf,))] + [dma((n,))] * 6,
        compiler_params=pltpu.CompilerParams(
            collective_id=0, has_side_effects=True, vmem_limit_bytes=48 * 2**20
        ),
        name="gather_kv",
    )(x, k, w_value)

    ids = jnp.concatenate([c[None].astype(jnp.int32), lax.dynamic_index_in_dim(picks, c, 0, False)])
    block = (1, BLOCK, HEAD)
    head = pl.BlockSpec((BLOCK, HEAD), lambda h, ids: (0, h))
    fixed2 = pl.BlockSpec((BLOCK, HEAD), lambda h, ids: (0, 0))
    pair = pl.BlockSpec((2, BLOCK, HEAD), lambda h, ids: (0, 0, 0))
    at = [pl.BlockSpec(block, lambda h, ids, j=j: (ids[j], 0, 0)) for j in range(3)]
    dq, own_k, own_v, slot_k, slot_v = pl.pallas_call(
        attend_kernel,
        out_shape=[
            jax.ShapeDtypeStruct((BLOCK, GROUP * HEAD), BF16),
            jax.ShapeDtypeStruct((BLOCK, HEAD), F32),
            jax.ShapeDtypeStruct((BLOCK, HEAD), F32),
            jax.ShapeDtypeStruct((2, BLOCK, HEAD), BF16),
            jax.ShapeDtypeStruct((2, BLOCK, HEAD), BF16),
        ],
        grid_spec=pltpu.PrefetchScalarGridSpec(
            num_scalar_prefetch=1,
            grid=(GROUP,),
            in_specs=[head, head, fixed2, at[1], at[2], at[0], at[1], at[2]],
            out_specs=[head, fixed2, fixed2, pair, pair],
            scratch_shapes=[VM((3, BLOCK, HEAD), F32)] * 2,
        ),
        compiler_params=pltpu.CompilerParams(vmem_limit_bytes=48 * 2**20),
        name="attend",
    )(ids, q, g, k, kall, kall, vall, vall, vall)

    rows = x.shape[1] // (n * nf)
    line_buf = VM((lines, BLOCK, HEAD), BF16)
    gk, gv, gw = pl.pallas_call(
        lambda *refs: reduce_kernel(n, nf, *refs),
        out_shape=[
            jax.ShapeDtypeStruct((BLOCK, HEAD), BF16),
            jax.ShapeDtypeStruct((BLOCK, HEAD), BF16),
            jax.ShapeDtypeStruct((rows, HEAD), BF16),
        ],
        in_specs=[smem] + [vmem] * 5,
        out_specs=[vmem] * 3,
        scratch_shapes=[VM((2, BLOCK, HEAD), BF16)] * 2
        + [line_buf] * 4
        + [
            VM((nf, n, rows, HEAD), F32),
            VM((nf, n, rows, HEAD), BF16),
            VM((nf, n, rows, HEAD), BF16),
        ]
        + [VM((lines, rows, HEAD), BF16)] * 4
        + [
            dma((2,)), dma((2,)), dma((2, lines)), dma((2, lines)), dma((nf,)), dma((nf,)),
            dma((2,)), dma((lines,)), dma((lines,)),
        ],
        compiler_params=pltpu.CompilerParams(
            collective_id=1, has_side_effects=True, vmem_limit_bytes=56 * 2**20
        ),
        name="reduce_grads",
    )(picks, x, own_k, own_v, slot_k, slot_v)
    return dq[None], gk[None], gv[None], gw


def solution(mesh):
    in_specs = (
        P("fsdp", "ctx", None),
        P("fsdp", "ctx", None),
        P("fsdp", "ctx", None),
        P("fsdp", None),
        P("fsdp", "ctx", None),
        P("fsdp", None, None),
    )
    out_specs = (
        P("fsdp", "ctx", None),
        P("fsdp", "ctx", None),
        P("fsdp", "ctx", None),
        P(("ctx", "fsdp"), None),
    )
    return jax.shard_map(
        on_device, mesh=mesh, in_specs=in_specs, out_specs=out_specs, check_vma=False
    )
```

time: 301 us -> 120 us (0.40)
  waiting for transfers between devices: 123 us -> 0 us
  Pallas kernels: 0 us -> 106 us
  blocking collectives: 61.3 us -> 0 us
  matrix products: 55.4 us -> 0 us
  other arithmetic: 18.2 us -> 0.08 us
  local copies, waits for them, and re-layouts: 28 us -> 12.2 us
  between operations: 13.9 us -> 0.69 us
    pallas_call x0 -> x3, Pallas kernels: none -> 106 us  [the longest x1 70.9 us: on_device(): pl.pallas_call(lambda *refs: reduce_kernel(n, nf, *refs), out_shape=[jax....]
    reduce_scatter x1 -> x0, waiting for transfers between devices: 60.2 us -> none  [on_device(): lax.psum_scatter(jnp.einsum('tc,th->ch', columns, grad_value_rows, prefer...]
    dot_general x27 -> x0, matrix products: 55.4 us -> none  [the longest x4 10.8 us: head_pass(): jnp.dot(dscores, key_block, preferred_element_type=jnp.float32) * inv_root]
    all_to_all x1 -> x0, blocking collectives: 52.4 us -> none  [on_device(): lax.all_to_all(spread, 'ctx', split_axis=0, concat_axis=0, tiled=True)]
    all_gather x1 -> x0, waiting for transfers between devices: 43.8 us -> none  [on_device(): kv_piece = lax.all_gather(paired, 'ctx', axis=0, tiled=True)]
    unnamed x4 -> x0, waiting for transfers between devices: 19.3 us -> none
    all_gather x1 -> x0, blocking collectives: 8.96 us -> none  [on_device(): lax.all_gather(w_value, 'fsdp', axis=0, tiled=True)]
    reduce_sum x5 -> x0, other arithmetic: 6.47 us -> none  [the longest x4 4.44 us: head_pass(): weights = exp_terms / jnp.sum(exp_terms, axis=1, keepdims=True)]
  transfers between devices with their start and end apart: 3 -> 0, of which waited for: 3 -> 0; matrix products, arithmetic and copies ran while one was open for 3% -> 0% of each run, Pallas kernels for 0% -> 0%
where the time goes in v1:
time: 120 us; the launch traced here: 119 us
  Pallas kernels  106 us (88%)
  local copies, waits for them, and re-layouts  12.2 us (10%)
    pallas_call x1, Pallas kernels, on_device(): pl.pallas_call(lambda *refs: reduce_kernel(n, nf, *refs), out_shape=[jax....  70.9 us
    pallas_call x1, Pallas kernels, on_device(): pl.pallas_call(attend_kernel, out_shape=[jax.ShapeDtypeStruct((BLOCK, GRO...  19.6 us
    pallas_call x1, Pallas kernels, on_device(): pl.pallas_call(lambda *refs: gather_kernel(n, nf, *refs), out_shape=[jax....  15.7 us
    unnamed x23, local copies, waits for them, and re-layouts  10.7 us

profile of v1, /device:TPU:0, one launch (start us, length us, event | category | flops | bytes accessed | tf_op | source)
XLA Modules:
  0.0 119.2 jit_solution(11492842703611814821)
XLA Ops:
  0.6 0.9 dynamic-slice_reduce_fusion
  1.5 0.1 pad_add_fusion.ids
  1.6 0.0 copy-start
  1.6 1.6 %copy-done = bf16[1,512,2048]{2,1,0:T(8,128)(2,1)S(1)} copy-done((bf16[1,512,2048]{2,1,0:T(8,128)(2,1)S(1)}, bf16[1,512,2048]{2,1,0:T(8,128)(2,1)}, u32[]{:S(2)}) %copy-start) | copy-done | bytes 2097176
  3.2 0.0 copy-start.3
  3.2 0.9 copy-done.3
  4.1 0.0 copy-start.8
  4.1 0.9 copy-done.8
  5.0 0.0 copy-start.1
  5.0 15.7 %gather_kv.1 = (bf16[8,512,128]{2,1,0:T(8,128)(2,1)S(1)}, bf16[8,512,128]{2,1,0:T(8,128)(2,1)S(1)}) custom-call(bf16[512,2048]{1,0:T(8,128)(2,1)S(1)} %bitcast.10, bf16[512,128]{1,0:T(8,128)(2,1)S(1)} %bitcast.13, bf16[512,128]{1,0:T(8,128)(2,1)S(1)} %copy-done.8), custom_call_target="tpu_custom_call" | custom-call | tf_op jit(solution)/shard_map/gather_kv/pallas_call | solution.py:370
  20.7 0.0 copy-done.1
  20.8 0.0 copy-done.2
  20.8 0.0 copy-start.9
  20.8 19.6 %attend.1 = (bf16[512,512]{1,0:T(8,128)(2,1)}, f32[512,128]{1,0:T(8,128)S(1)}, f32[512,128]{1,0:T(8,128)S(1)}, bf16[2,512,128]{2,1,0:T(8,128)(2,1)S(1)}, bf16[2,512,128]{2,1,0:T(8,128)(2,1)S(1)}) custom-call(s32[3]{0:T(128)S(1)} %pad_add_fusion.ids, bf16[512,512]{1,0:T(8,128)(2,1)S(1)} %bitcast.11, bf16[512,512]{1,0:T(8,128)(2,1)S(1)} %bitcast.12, ...), custom_call_target="tpu_custom_call" | custom-call | tf_op jit(solution)/shard_map/attend/pallas_call | solution.py:388
  40.4 0.7 copy-done.4
  41.1 0.7 copy-done.5
  41.8 0.7 copy-done.6
  42.5 0.7 copy-done.7
  43.2 0.0 copy-done.9
  43.2 0.7 copy.10.refs_0_
  43.9 70.9 %reduce_grads.1 = (bf16[512,128]{1,0:T(8,128)(2,1)}, bf16[512,128]{1,0:T(8,128)(2,1)}, bf16[64,128]{1,0:T(8,128)(2,1)}) custom-call(s32[8,2]{1,0:T(8,128)} %copy.10.refs_0_, bf16[512,2048]{1,0:T(8,128)(2,1)} %bitcast.9, f32[512,128]{1,0:T(8,128)} %copy-done.4, f32[512,128]{1,0:T(8,128)} %copy-done.5, bf16[2,512,128]{2,1,0:T(8,128)(2,1)} %copy-done.6, ...), custom_call_target="tpu_custom_call" | custom-call | tf_op jit(solution)/shard_map/reduce_grads/pallas_call | solution.py:410
  114.8 1.6 %copy.14 = bf16[1,512,128]{2,1,0:T(8,128)(2,1)} copy(bf16[1,512,128]{2,1,0:T(8,128)(2,1)} %bitcast.16) | data formatting | bytes 262144
  116.3 1.6 %copy.15 = bf16[1,512,128]{2,1,0:T(8,128)(2,1)} copy(bf16[1,512,128]{2,1,0:T(8,128)(2,1)} %bitcast.15) | data formatting | bytes 262144
  117.9 1.3 %copy.16 = bf16[64,128]{1,0:T(8,128)(2,1)} copy(bf16[64,128]{1,0:T(8,128)(2,1)} %get-tuple-element.31) | data formatting | bytes 32768
  (5 shorter events, 0.0 us)
Async XLA Ops:
  1.6 1.6 %copy-start = (bf16[1,512,2048]{2,1,0:T(8,128)(2,1)S(1)}, bf16[1,512,2048]{2,1,0:T(8,128)(2,1)}, u32[]{:S(2)}) copy-start(bf16[1,512,2048]{2,1,0:T(8,128)(2,1)} %param.6) | copy-start | bytes 6291460
  3.2 0.9 copy-start.3
  4.1 0.9 copy-start.8
  5.0 15.8 %copy-start.1 = (bf16[1,512,512]{2,1,0:T(8,128)(2,1)S(1)}, bf16[1,512,512]{2,1,0:T(8,128)(2,1)}, u32[]{:S(2)}) copy-start(bf16[1,512,512]{2,1,0:T(8,128)(2,1)} %param.7) | copy-start | bytes 1572868
  5.0 15.8 %copy-start.2 = (bf16[1,512,512]{2,1,0:T(8,128)(2,1)S(1)}, bf16[1,512,512]{2,1,0:T(8,128)(2,1)}, u32[]{:S(2)}) copy-start(bf16[1,512,512]{2,1,0:T(8,128)(2,1)} %param.10) | copy-start | bytes 1572868
  20.8 22.4 %copy-start.9 = (s32[1,8,2]{1,2,0:T(2,128)S(1)}, s32[1,8,2]{1,2,0:T(2,128)}, u32[]{:S(2)}) copy-start(s32[1,8,2]{1,2,0:T(2,128)} %param.11) | copy-start | bytes 196
  40.4 0.7 copy-start.4
  41.1 0.7 copy-start.5
  41.8 0.7 copy-start.6
  42.5 0.7 copy-start.7

commit v2 on v1

--- a/solution.py
+++ b/solution.py
@@ -80,17 +80,24 @@
 
 
 def gather_kernel(
-    n, nf, x_ref, k_ref, w_ref, kall, vall, wbuf, w_send, w_recv,
+    n, nf, x_hbm, k_hbm, w_hbm, kall, vall, x_ref, wbuf, load, w_send, w_recv,
     kz_send, vz_send, ky_send, vy_send, k_recv, v_recv,
 ):
     c, f = lax.axis_index("ctx"), lax.axis_index("fsdp")
     lines = n // 2
     y, z = c % 2, c // 2
     partner = 2 * z + (1 - y)
-    ws = w_ref.shape[0]
-    wbuf[f] = w_ref[...]
-    kall[c] = k_ref[...]
+    ws = w_hbm.shape[0]
+    loads = [
+        pltpu.make_async_copy(w_hbm, wbuf.at[f], load.at[0]),
+        pltpu.make_async_copy(k_hbm, kall.at[c], load.at[1]),
+        pltpu.make_async_copy(x_hbm, x_ref, load.at[2]),
+    ]
+    for copy in loads:
+        copy.start()
     greet(n, nf, True)
+    loads[0].wait()
+    loads[1].wait()
 
     def up(buf, b, send, recv):
         return remote(buf.at[b], buf.at[b], send.at[b], recv.at[b], ctx=c + 2)
@@ -138,11 +145,23 @@
         term = jnp.dot(x_ref[:, columns], wbuf[g], preferred_element_type=F32)
         return term if total is None else total + term
 
+    def relay(buf, s, zsend, ysend, recv):
+        b = c - 2 * s
+
+        @pl.when(z - s >= 0)
+        def _():
+            up(buf, b, zsend, recv).wait_recv()
+            forward(buf, b, zsend, ysend, recv, False)
+
+    early = 1
     for index in range(len(stages)):
         copies, came, slot = w_stage(index, held, slot)
         if index == 0:
             forward(kall, c, kz_send, ky_send, k_recv, True)
+            loads[2].wait()
             total = add(total, f)
+            for s in range(1, 1 + early):
+                relay(kall, s, kz_send, ky_send, k_recv)
         for copy in copies:
             copy.wait()
         held = held + came
@@ -152,14 +171,9 @@
     forward(vall, c, vz_send, vy_send, v_recv, True)
 
     for s in range(1, lines):
-        b = c - 2 * s
-
-        @pl.when(z - s >= 0)
-        def _():
-            up(kall, b, kz_send, k_recv).wait_recv()
-            forward(kall, b, kz_send, ky_send, k_recv, False)
-            up(vall, b, vz_send, v_recv).wait_recv()
-            forward(vall, b, vz_send, vy_send, v_recv, False)
+        if s + early < lines:
+            relay(kall, s + early, kz_send, ky_send, k_recv)
+        relay(vall, s, vz_send, vy_send, v_recv)
 
     @pl.when(y == 1)
     def _():
@@ -193,7 +207,7 @@
 
 
 def attend_kernel(
-    ids, q_ref, g_ref, k0, k1, k2, v0, v1, v2, dq_ref, own_k, own_v, slot_k, slot_v, dk_acc, dv_acc
+    me, picks, q_ref, g_ref, k0, k1, k2, v0, v1, v2, dq_ref, own_k, own_v, slot_k, slot_v, dk_acc, dv_acc
 ):
     h = pl.program_id(0)
     inv_root = 1.0 / math.sqrt(HEAD)
@@ -203,26 +217,29 @@
     vs = [v0[0], v1[0], v2[0]]
     nt = (((1,), (1,)), ((), ()))
     tn = (((0,), (0,)), ((), ()))
-    scores = []
+    scale = inv_root / math.log(2.0)
+    scores, tops = [], []
     for j in range(3):
-        s = lax.dot_general(ks[j], q, nt, preferred_element_type=F32) * inv_root
+        s = lax.dot_general(ks[j], q, nt, preferred_element_type=F32)
         if j == 0:
             u = lax.broadcasted_iota(jnp.int32, s.shape, 0)
             t = lax.broadcasted_iota(jnp.int32, s.shape, 1)
             s = jnp.where(u <= t, s, NEG)
-        else:
-            s = jnp.where(ids[j] != ids[0], s, NEG)
         scores.append(s)
-    highest = jnp.max(
-        jnp.maximum(jnp.maximum(scores[0], scores[1]), scores[2]), axis=0, keepdims=True
-    )
-    exps = [jnp.exp(s - highest) for s in scores]
-    norm = 1.0 / jnp.sum(exps[0] + exps[1] + exps[2], axis=0, keepdims=True)
+        tops.append(jnp.max(s, axis=0, keepdims=True))
+    use = [picks[me[0], j] != me[0] for j in range(2)]
+    highest = tops[0]
+    for j in range(2):
+        highest = jnp.maximum(highest, jnp.where(use[j], tops[j + 1], NEG))
+    highest = highest * scale
+    shifts = [highest] + [jnp.where(use[j], highest, -NEG) for j in range(2)]
+    exps = [jnp.exp2(s * scale - shift) for s, shift in zip(scores, shifts)]
+    norm = 1.0 / sum(jnp.sum(e, axis=0, keepdims=True) for e in exps)
     weights = [e * norm for e in exps]
     lows = [w.astype(BF16) for w in weights]
     dws = [lax.dot_general(v, g, nt, preferred_element_type=F32) for v in vs]
-    delta = jnp.sum(
-        sum(low.astype(F32) * dw for low, dw in zip(lows, dws)), axis=0, keepdims=True
+    delta = sum(
+        jnp.sum(low.astype(F32) * dw, axis=0, keepdims=True) for low, dw in zip(lows, dws)
     )
     ds = [(w * (dw - delta)).astype(BF16) for w, dw in zip(weights, dws)]
     dq = sum(lax.dot_general(d, k, tn, preferred_element_type=F32) for d, k in zip(ds, ks))
@@ -247,14 +264,16 @@
 
 
 def reduce_kernel(
-    n, nf, picks, x_ref, own_k, own_v, slot_k, slot_v, gk_ref, gv_ref, gw_ref,
+    n, nf, picks, x_hbm, own_k, own_v, slot_k, slot_v, gk_ref, gv_ref, gw_ref,
     pslot_k, pslot_v, sbuf_k, sbuf_v, rbuf_k, rbuf_v, acc, wsend, wrecv, ysend_buf, yrecv_buf,
-    zsend_buf, zrecv_buf, p_send, p_recv, c_send, c_recv, f_send, f_recv, y_sem, z_send, z_recv,
+    zsend_buf, zrecv_buf, x_ref, xt, load, p_send, p_recv, c_send, c_recv, f_send, f_recv, y_sem, z_send, z_recv,
 ):
     c, f = lax.axis_index("ctx"), lax.axis_index("fsdp")
     lines = n // 2
     y, z = c % 2, c // 2
     partner = 2 * z + (1 - y)
+    fetch = pltpu.make_async_copy(x_hbm, x_ref, load.at[0])
+    fetch.start()
     greet(n, nf, True)
     sides = []
     for side, (slots, pslots) in enumerate(((slot_v, pslot_v), (slot_k, pslot_k))):
@@ -262,50 +281,59 @@
         copy.start()
         sides.append(copy)
 
-    def chain(side):
+    fetch.wait()
+    xt[...] = x_ref[...].T
+
+    def down(side, zd):
+        sbuf, rbuf = ((sbuf_v, rbuf_v), (sbuf_k, rbuf_k))[side]
+        return remote(
+            sbuf.at[zd], rbuf.at[zd], c_send.at[side, zd], c_recv.at[side, zd], ctx=c - 2
+        )
+
+    def step(side, zd):
         own, slots, pslots, sbuf, rbuf, out = (
             (own_v, slot_v, pslot_v, sbuf_v, rbuf_v, gv_ref),
             (own_k, slot_k, pslot_k, sbuf_k, rbuf_k, gk_ref),
         )[side]
 
-        def down(zd):
-            return remote(
-                sbuf.at[zd], rbuf.at[zd], c_send.at[side, zd], c_recv.at[side, zd], ctx=c - 2
-            )
-
-        sides[side].wait()
-        for zd in range(lines):
-            @pl.when(zd <= z)
+        @pl.when(zd <= z)
+        def _():
+            dest = 2 * zd + y
+            value = jnp.zeros(own.shape, F32)
+            for owner, held in ((c, slots), (partner, pslots)):
+                for j in range(2):
+                    gate = jnp.where(picks[owner, j] == dest, 1.0, 0.0).astype(F32)
+                    value = value + held[j].astype(F32) * gate
+            sbuf[zd] = value.astype(BF16)
+
+            @pl.when(z < lines - 1)
             def _():
-                dest = 2 * zd + y
-                value = jnp.zeros(own.shape, F32)
-                for owner, held in ((c, slots), (partner, pslots)):
-                    for j in range(2):
-                        gate = jnp.where(picks[owner, j] == dest, 1.0, 0.0).astype(F32)
-                        value = value + held[j].astype(F32) * gate
-                sbuf[zd] = value.astype(BF16)
-
-                @pl.when(z < lines - 1)
-                def _():
-                    down(zd).wait_recv()
-                    sbuf[zd] = (value + rbuf[zd].astype(F32)).astype(BF16)
-
-                @pl.when(zd < z)
-                def _():
-                    down(zd).start()
-
-                @pl.when(zd == z)
-                def _():
-                    out[...] = (sbuf[zd].astype(F32) + own[...]).astype(BF16)
-
-        return down
-
-    down_v = chain(0)
+                down(side, zd).wait_recv()
+                sbuf[zd] = (value + rbuf[zd].astype(F32)).astype(BF16)
+
+            @pl.when(zd < z)
+            def _():
+                down(side, zd).start()
+
+            @pl.when(zd == z)
+            def _():
+                out[...] = (sbuf[zd].astype(F32) + own[...]).astype(BF16)
+
+    later = list(range(lines))
+
+    def key_step():
+        if later:
+            if len(later) == lines:
+                sides[1].wait()
+            step(1, later.pop(0))
+
+    sides[0].wait()
+    for zd in range(lines):
+        step(0, zd)
     gv = gv_ref[...]
     rows = x_ref.shape[1] // (n * nf)
     group = x_ref.shape[1] // n
-    tn = (((0,), (0,)), ((), ()))
-    part = lax.dot_general(x_ref[...], gv, tn, preferred_element_type=F32)
+    part = jnp.dot(xt[...], gv, preferred_element_type=F32)
     for cc in range(n):
         for ff in range(nf):
             at = cc * group + ff * rows
@@ -327,6 +355,7 @@
             copy.start()
             now.append((copy, hi * 2 * bit + mine * bit + low, slot))
             slot += 1
+        key_step()
         for copy, keep, at in now:
             copy.wait()
             acc[keep] += wrecv[at].astype(F32)
@@ -334,6 +363,7 @@
         ysend_buf[zz] = acc[f, 2 * zz + (1 - y)].astype(BF16)
     copy = remote(ysend_buf, yrecv_buf, y_sem.at[0], y_sem.at[1], ctx=partner)
     copy.start()
+    key_step()
     copy.wait()
     now = []
     for o in range(1, lines):
@@ -344,18 +374,25 @@
         )
         copy.start()
         now.append(copy)
+    while later:
+        key_step()
     total = acc[f, c] + yrecv_buf[z].astype(F32)
     for o, copy in enumerate(now):
         copy.wait()
         total = total + zrecv_buf[o + 1].astype(F32)
     gw_ref[...] = total.astype(BF16)
 
-    down_k = chain(1)
     for zd in range(lines):
         @pl.when(zd < z)
         def _():
-            down_v(zd).wait_send()
-            down_k(zd).wait_send()
+            down(0, zd).wait_send()
+            down(1, zd).wait_send()
+
+
+def finish_kernel(gk, gv, gw, gk_out, gv_out, gw_out):
+    gk_out[...] = gk[...]
+    gv_out[...] = gv[...]
+    gw_out[...] = gw[...]
 
 
 def on_device(inputs, queries, key_vectors, w_value, grad_out, block_picks):
@@ -365,26 +402,29 @@
     x, q, k, g, picks = inputs[0], queries[0], key_vectors[0], grad_out[0], block_picks[0]
     dma = pltpu.SemaphoreType.DMA
     vmem = pl.BlockSpec(memory_space=VM)
+    hbm = pl.BlockSpec(memory_space=pltpu.HBM)
     smem = pl.BlockSpec(memory_space=pltpu.SMEM)
     ws = w_value.shape[0]
     kall, vall = pl.pallas_call(
         lambda *refs: gather_kernel(n, nf, *refs),
         out_shape=[jax.ShapeDtypeStruct((n, BLOCK, HEAD), BF16)] * 2,
-        in_specs=[vmem] * 3,
+        in_specs=[hbm] * 3,
         out_specs=[vmem] * 2,
-        scratch_shapes=[VM((nf, ws, HEAD), BF16), dma((nf,)), dma((nf,))] + [dma((n,))] * 6,
+        scratch_shapes=[VM(x.shape, BF16), VM((nf, ws, HEAD), BF16), dma((3,)), dma((nf,)), dma((nf,))] + [dma((n,))] * 6,
         compiler_params=pltpu.CompilerParams(
-            collective_id=0, has_side_effects=True, vmem_limit_bytes=48 * 2**20
+            collective_id=0, has_side_effects=True, vmem_limit_bytes=58 * 2**20
         ),
         name="gather_kv",
     )(x, k, w_value)
 
-    ids = jnp.concatenate([c[None].astype(jnp.int32), lax.dynamic_index_in_dim(picks, c, 0, False)])
+    me = c[None].astype(jnp.int32)
     block = (1, BLOCK, HEAD)
-    head = pl.BlockSpec((BLOCK, HEAD), lambda h, ids: (0, h))
-    fixed2 = pl.BlockSpec((BLOCK, HEAD), lambda h, ids: (0, 0))
-    pair = pl.BlockSpec((2, BLOCK, HEAD), lambda h, ids: (0, 0, 0))
-    at = [pl.BlockSpec(block, lambda h, ids, j=j: (ids[j], 0, 0)) for j in range(3)]
+    head = pl.BlockSpec((BLOCK, HEAD), lambda h, me, picks: (0, h))
+    fixed2 = pl.BlockSpec((BLOCK, HEAD), lambda h, me, picks: (0, 0))
+    pair = pl.BlockSpec((2, BLOCK, HEAD), lambda h, me, picks: (0, 0, 0))
+    at = [pl.BlockSpec(block, lambda h, me, picks: (me[0], 0, 0))]
+    for j in range(2):
+        at.append(pl.BlockSpec(block, lambda h, me, picks, j=j: (picks[me[0], j], 0, 0)))
     dq, own_k, own_v, slot_k, slot_v = pl.pallas_call(
         attend_kernel,
         out_shape=[
@@ -395,15 +435,15 @@
             jax.ShapeDtypeStruct((2, BLOCK, HEAD), BF16),
         ],
         grid_spec=pltpu.PrefetchScalarGridSpec(
-            num_scalar_prefetch=1,
+            num_scalar_prefetch=2,
             grid=(GROUP,),
             in_specs=[head, head, fixed2, at[1], at[2], at[0], at[1], at[2]],
             out_specs=[head, fixed2, fixed2, pair, pair],
             scratch_shapes=[VM((3, BLOCK, HEAD), F32)] * 2,
         ),
-        compiler_params=pltpu.CompilerParams(vmem_limit_bytes=48 * 2**20),
+        compiler_params=pltpu.CompilerParams(vmem_limit_bytes=40 * 2**20),
         name="attend",
-    )(ids, q, g, k, kall, kall, vall, vall, vall)
+    )(me, picks, q, g, k, kall, kall, vall, vall, vall)
 
     rows = x.shape[1] // (n * nf)
     line_buf = VM((lines, BLOCK, HEAD), BF16)
@@ -414,7 +454,7 @@
             jax.ShapeDtypeStruct((BLOCK, HEAD), BF16),
             jax.ShapeDtypeStruct((rows, HEAD), BF16),
         ],
-        in_specs=[smem] + [vmem] * 5,
+        in_specs=[smem, hbm] + [vmem] * 4,
         out_specs=[vmem] * 3,
         scratch_shapes=[VM((2, BLOCK, HEAD), BF16)] * 2
         + [line_buf] * 4
@@ -424,15 +464,24 @@
             VM((nf, n, rows, HEAD), BF16),
         ]
         + [VM((lines, rows, HEAD), BF16)] * 4
+        + [VM(x.shape, BF16), VM(x.shape[::-1], BF16), dma((1,))]
         + [
             dma((2,)), dma((2,)), dma((2, lines)), dma((2, lines)), dma((nf,)), dma((nf,)),
             dma((2,)), dma((lines,)), dma((lines,)),
         ],
         compiler_params=pltpu.CompilerParams(
-            collective_id=1, has_side_effects=True, vmem_limit_bytes=56 * 2**20
+            collective_id=1, has_side_effects=True, vmem_limit_bytes=32 * 2**20
         ),
         name="reduce_grads",
     )(picks, x, own_k, own_v, slot_k, slot_v)
+    gk, gv, gw = pl.pallas_call(
+        finish_kernel,
+        out_shape=[jax.ShapeDtypeStruct(a.shape, BF16) for a in (gk, gv, gw)],
+        in_specs=[vmem] * 3,
+        out_specs=[vmem] * 3,
+        compiler_params=pltpu.CompilerParams(vmem_limit_bytes=4 * 2**20),
+        name="finish",
+    )(gk, gv, gw)
     return dq[None], gk[None], gv[None], gw
 
 

time: 120 us -> 97.5 us (0.81)
  Pallas kernels: 106 us -> 93.2 us
  local copies, waits for them, and re-layouts: 12.2 us -> 3.3 us
    pallas_call x1, Pallas kernels: 70.9 us -> 56.1 us  [on_device(): pl.pallas_call(lambda *refs: reduce_kernel(n, nf, *refs), out_shape=[jax....]
    unnamed x23 -> x12, local copies, waits for them, and re-layouts: 10.7 us -> 2.46 us
    pallas_call x1, Pallas kernels: 15.7 us -> 17.1 us  [on_device(): pl.pallas_call(lambda *refs: gather_kernel(n, nf, *refs), out_shape=[jax....]
where the time goes in v2:
time: 97.5 us; the launch traced here: 97.3 us
  Pallas kernels  93.2 us (96%)
  local copies, waits for them, and re-layouts  3.3 us (3%)
    pallas_call x1, Pallas kernels, on_device(): pl.pallas_call(lambda *refs: reduce_kernel(n, nf, *refs), out_shape=[jax....  56.1 us
    pallas_call x1, Pallas kernels, on_device(): pl.pallas_call(attend_kernel, out_shape=[jax.ShapeDtypeStruct((BLOCK, GRO...  19.3 us
    pallas_call x1, Pallas kernels, on_device(): pl.pallas_call(lambda *refs: gather_kernel(n, nf, *refs), out_shape=[jax....  17.1 us
    unnamed x12, local copies, waits for them, and re-layouts  2.46 us

profile of v2, /device:TPU:0, one launch (start us, length us, event | category | flops | bytes accessed | tf_op | source)
XLA Modules:
  0.0 97.3 jit_solution(10143925168141053423)
XLA Ops:
  0.6 0.0 copy-start.4
  0.6 0.0 copy-start.5
  0.7 0.0 copy-start.3
  0.7 0.8 copy.10.picks.refs_0_
  1.5 17.1 %gather_kv.1 = (bf16[8,512,128]{2,1,0:T(8,128)(2,1)}, bf16[8,512,128]{2,1,0:T(8,128)(2,1)}) custom-call(bf16[512,2048]{1,0:T(8,128)(2,1)} %bitcast.9, bf16[512,128]{1,0:T(8,128)(2,1)} %bitcast.13, bf16[512,128]{1,0:T(8,128)(2,1)} %refs_2_.1), custom_call_target="tpu_custom_call" | custom-call | tf_op jit(solution)/shard_map/gather_kv/pallas_call | solution.py:408
  18.6 0.0 copy-done.4
  18.6 0.0 copy-done.5
  18.6 0.0 copy-done.3
  18.6 0.0 copy-start
  18.6 1.2 %copy-done = bf16[8,512,128]{2,1,0:T(8,128)(2,1)S(1)} copy-done((bf16[8,512,128]{2,1,0:T(8,128)(2,1)S(1)}, bf16[8,512,128]{2,1,0:T(8,128)(2,1)}, u32[]{:S(2)}) %copy-start) | copy-done | bytes 1048600
  19.8 0.0 copy-start.2
  19.8 1.2 %copy-done.2 = bf16[8,512,128]{2,1,0:T(8,128)(2,1)S(1)} copy-done((bf16[8,512,128]{2,1,0:T(8,128)(2,1)S(1)}, bf16[8,512,128]{2,1,0:T(8,128)(2,1)}, u32[]{:S(2)}) %copy-start.2) | copy-done | bytes 1048600
  21.1 0.0 copy-start.1
  21.1 19.3 %attend.1 = (bf16[512,512]{1,0:T(8,128)(2,1)}, f32[512,128]{1,0:T(8,128)S(1)}, f32[512,128]{1,0:T(8,128)S(1)}, bf16[2,512,128]{2,1,0:T(8,128)(2,1)S(1)}, bf16[2,512,128]{2,1,0:T(8,128)(2,1)S(1)}) custom-call(s32[1]{0:T(128)} %bitcast.me, s32[8,2]{1,0:T(8,128)S(1)} %copy.10.picks.refs_0_, bf16[512,512]{1,0:T(8,128)(2,1)S(1)} %bitcast.11, ...), custom_call_target="tpu_custom_call" | custom-call | tf_op jit(solution)/shard_map/attend/pallas_call | solution.py:428
  40.4 0.0 copy-done.1
  40.4 56.1 %reduce_grads.1 = (bf16[512,128]{1,0:T(8,128)(2,1)S(1)}, bf16[512,128]{1,0:T(8,128)(2,1)S(1)}, bf16[64,128]{1,0:T(8,128)(2,1)S(1)}) custom-call(s32[8,2]{1,0:T(8,128)S(1)} %copy.10.picks.refs_0_, bf16[512,2048]{1,0:T(8,128)(2,1)S(1)} %bitcast.10, f32[512,128]{1,0:T(8,128)S(1)} %get-tuple-element.20.refs_2_, f32[512,128]{1,0:T(8,128)S(1)} %get-tuple-element.21.refs_3_, ...), custom_call_target="tpu_custom_call" | custom-call | tf_op jit(solution)/shard_map/reduce_grads/pallas_call | solution.py:450
  96.5 0.7 finish.1
Async XLA Ops:
  0.6 18.0 %copy-start.4 = (bf16[1,512,512]{2,1,0:T(8,128)(2,1)S(1)}, bf16[1,512,512]{2,1,0:T(8,128)(2,1)}, u32[]{:S(2)}) copy-start(bf16[1,512,512]{2,1,0:T(8,128)(2,1)} %param.10) | copy-start | bytes 1572868
  0.6 18.0 %copy-start.5 = (bf16[1,512,128]{2,1,0:T(8,128)(2,1)S(1)}, bf16[1,512,128]{2,1,0:T(8,128)(2,1)}, u32[]{:S(2)}) copy-start(bf16[1,512,128]{2,1,0:T(8,128)(2,1)} %param.8) | copy-start | bytes 393220
  0.7 18.0 %copy-start.3 = (bf16[1,512,512]{2,1,0:T(8,128)(2,1)S(1)}, bf16[1,512,512]{2,1,0:T(8,128)(2,1)}, u32[]{:S(2)}) copy-start(bf16[1,512,512]{2,1,0:T(8,128)(2,1)} %param.7) | copy-start | bytes 1572868
  18.6 1.2 %copy-start = (bf16[8,512,128]{2,1,0:T(8,128)(2,1)S(1)}, bf16[8,512,128]{2,1,0:T(8,128)(2,1)}, u32[]{:S(2)}) copy-start(bf16[8,512,128]{2,1,0:T(8,128)(2,1)} %get-tuple-element.18.v0.v1.v2) | copy-start | bytes 3145732
  19.8 1.2 %copy-start.2 = (bf16[8,512,128]{2,1,0:T(8,128)(2,1)S(1)}, bf16[8,512,128]{2,1,0:T(8,128)(2,1)}, u32[]{:S(2)}) copy-start(bf16[8,512,128]{2,1,0:T(8,128)(2,1)} %get-tuple-element.17.k1.k2) | copy-start | bytes 3145732
  21.1 19.3 %copy-start.1 = (bf16[1,512,2048]{2,1,0:T(8,128)(2,1)S(1)}, bf16[1,512,2048]{2,1,0:T(8,128)(2,1)}, u32[]{:S(2)}) copy-start(bf16[1,512,2048]{2,1,0:T(8,128)(2,1)} %param.6) | copy-start | bytes 6291460

commit v3 on v2

--- a/solution.py
+++ b/solution.py
@@ -36,7 +36,7 @@
     )
 
 
-def greet(n, nf, direct):
+def greet(n, nf):
     c, f = lax.axis_index("ctx"), lax.axis_index("fsdp")
     lines = n // 2
     y, z = c % 2, c // 2
@@ -52,31 +52,12 @@
         barrier, inc=1, device_id={"ctx": 2 * z + (1 - y)}, device_id_type=MESH
     )
     count += 1
-    if direct:
-        for o in range(1, lines):
-            pl.semaphore_signal(
-                barrier, inc=1, device_id={"ctx": 2 * ((z + o) % lines) + y}, device_id_type=MESH
-            )
-            count += 1
-        pl.semaphore_wait(barrier, count)
-    else:
-        pl.semaphore_wait(barrier, count)
-
-        @pl.when(z > 0)
-        def _():
-            pl.semaphore_signal(barrier, inc=1, device_id={"ctx": c - 2}, device_id_type=MESH)
-
-        @pl.when(z < lines - 1)
-        def _():
-            pl.semaphore_signal(barrier, inc=1, device_id={"ctx": c + 2}, device_id_type=MESH)
-
-        @pl.when(z > 0)
-        def _():
-            pl.semaphore_wait(barrier, 1)
-
-        @pl.when(z < lines - 1)
-        def _():
-            pl.semaphore_wait(barrier, 1)
+    for o in range(1, lines):
+        pl.semaphore_signal(
+            barrier, inc=1, device_id={"ctx": 2 * ((z + o) % lines) + y}, device_id_type=MESH
+        )
+        count += 1
+    return lambda: pl.semaphore_wait(barrier, count)
 
 
 def gather_kernel(
@@ -95,7 +76,7 @@
     ]
     for copy in loads:
         copy.start()
-    greet(n, nf, True)
+    greet(n, nf)()
     loads[0].wait()
     loads[1].wait()
 
@@ -206,83 +187,66 @@
                 done()
 
 
-def attend_kernel(
-    me, picks, q_ref, g_ref, k0, k1, k2, v0, v1, v2, dq_ref, own_k, own_v, slot_k, slot_v, dk_acc, dv_acc
-):
-    h = pl.program_id(0)
-    inv_root = 1.0 / math.sqrt(HEAD)
-    q = q_ref[...]
-    g = g_ref[...]
-    ks = [k0[...], k1[0], k2[0]]
-    vs = [v0[0], v1[0], v2[0]]
-    nt = (((1,), (1,)), ((), ()))
-    tn = (((0,), (0,)), ((), ()))
-    scale = inv_root / math.log(2.0)
-    scores, tops = [], []
-    for j in range(3):
-        s = lax.dot_general(ks[j], q, nt, preferred_element_type=F32)
-        if j == 0:
-            u = lax.broadcasted_iota(jnp.int32, s.shape, 0)
-            t = lax.broadcasted_iota(jnp.int32, s.shape, 1)
-            s = jnp.where(u <= t, s, NEG)
-        scores.append(s)
-        tops.append(jnp.max(s, axis=0, keepdims=True))
-    use = [picks[me[0], j] != me[0] for j in range(2)]
-    highest = tops[0]
-    for j in range(2):
-        highest = jnp.maximum(highest, jnp.where(use[j], tops[j + 1], NEG))
-    highest = highest * scale
-    shifts = [highest] + [jnp.where(use[j], highest, -NEG) for j in range(2)]
-    exps = [jnp.exp2(s * scale - shift) for s, shift in zip(scores, shifts)]
-    norm = 1.0 / sum(jnp.sum(e, axis=0, keepdims=True) for e in exps)
-    weights = [e * norm for e in exps]
-    lows = [w.astype(BF16) for w in weights]
-    dws = [lax.dot_general(v, g, nt, preferred_element_type=F32) for v in vs]
-    delta = sum(
-        jnp.sum(low.astype(F32) * dw, axis=0, keepdims=True) for low, dw in zip(lows, dws)
-    )
-    ds = [(w * (dw - delta)).astype(BF16) for w, dw in zip(weights, dws)]
-    dq = sum(lax.dot_general(d, k, tn, preferred_element_type=F32) for d, k in zip(ds, ks))
-    dq_ref[...] = (dq * inv_root).astype(BF16)
-
-    @pl.when(h == 0)
-    def _():
-        dk_acc[...] = jnp.zeros_like(dk_acc)
-        dv_acc[...] = jnp.zeros_like(dv_acc)
-
-    for j in range(3):
-        dk_acc[j] += jnp.dot(ds[j], q, preferred_element_type=F32)
-        dv_acc[j] += jnp.dot(lows[j], g, preferred_element_type=F32)
-
-    @pl.when(h == GROUP - 1)
-    def _():
-        own_k[...] = dk_acc[0] * inv_root
-        own_v[...] = dv_acc[0]
-        for j in (1, 2):
-            slot_k[j - 1] = (dk_acc[j] * inv_root).astype(BF16)
-            slot_v[j - 1] = dv_acc[j].astype(BF16)
-
-
 def reduce_kernel(
-    n, nf, picks, x_hbm, own_k, own_v, slot_k, slot_v, gk_ref, gv_ref, gw_ref,
+    n, nf, picks, x_ref, q_ref, g_ref, kall, vall, dq_ref, gk_ref, gv_ref, gw_ref,
+    ksel, vsel, ktr, lows, dk_acc, dv_acc, slot_k, slot_v,
     pslot_k, pslot_v, sbuf_k, sbuf_v, rbuf_k, rbuf_v, acc, wsend, wrecv, ysend_buf, yrecv_buf,
-    zsend_buf, zrecv_buf, x_ref, xt, load, p_send, p_recv, c_send, c_recv, f_send, f_recv, y_sem, z_send, z_recv,
+    zsend_buf, zrecv_buf, xt, p_send, p_recv, c_send, c_recv, f_send, f_recv, y_sem, z_send, z_recv,
 ):
     c, f = lax.axis_index("ctx"), lax.axis_index("fsdp")
     lines = n // 2
     y, z = c % 2, c // 2
     partner = 2 * z + (1 - y)
-    fetch = pltpu.make_async_copy(x_hbm, x_ref, load.at[0])
-    fetch.start()
-    greet(n, nf, True)
+    entered = greet(n, nf)
+    inv_root = 1.0 / math.sqrt(HEAD)
+    scale = inv_root / math.log(2.0)
+    nt = (((1,), (1,)), ((), ()))
+    ksel[0] = kall[c]
+    vsel[0] = vall[c]
+    for j in range(2):
+        ksel[j + 1] = kall[picks[c, j]]
+        vsel[j + 1] = vall[picks[c, j]]
+    for j in range(3):
+        ktr[j] = ksel[j].T
+    use = [picks[c, j] != c for j in range(2)]
+    dk_acc[...] = jnp.zeros_like(dk_acc)
+    dv_acc[...] = jnp.zeros_like(dv_acc)
+
+    def columns(h):
+        return pl.ds(pl.multiple_of(h * HEAD, HEAD), HEAD)
+
+    def value_pass(h, carry):
+        q, g = q_ref[:, columns(h)], g_ref[:, columns(h)]
+        scores, tops = [], []
+        for j in range(3):
+            s = lax.dot_general(ksel[j], q, nt, preferred_element_type=F32)
+            if j == 0:
+                u = lax.broadcasted_iota(jnp.int32, s.shape, 0)
+                t = lax.broadcasted_iota(jnp.int32, s.shape, 1)
+                s = jnp.where(u <= t, s, NEG)
+            scores.append(s)
+            tops.append(jnp.max(s, axis=0, keepdims=True))
+        highest = tops[0]
+        for j in range(2):
+            highest = jnp.maximum(highest, jnp.where(use[j], tops[j + 1], NEG))
+        highest = highest * scale
+        shifts = [highest] + [jnp.where(use[j], highest, -NEG) for j in range(2)]
+        exps = [jnp.exp2(s * scale - shift) for s, shift in zip(scores, shifts)]
+        norm = 1.0 / sum(jnp.sum(e, axis=0, keepdims=True) for e in exps)
+        for j in range(3):
+            low = (exps[j] * norm).astype(BF16)
+            lows[h, j] = low
+            dv_acc[j] += jnp.dot(low, g, preferred_element_type=F32)
+        return carry
+
+    lax.fori_loop(0, GROUP, value_pass, 0)
+    for j in range(2):
+        slot_v[j] = dv_acc[j + 1].astype(BF16)
+    entered()
     sides = []
     for side, (slots, pslots) in enumerate(((slot_v, pslot_v), (slot_k, pslot_k))):
-        copy = remote(slots, pslots, p_send.at[side], p_recv.at[side], ctx=partner)
-        copy.start()
-        sides.append(copy)
-
-    fetch.wait()
-    xt[...] = x_ref[...].T
+        sides.append(remote(slots, pslots, p_send.at[side], p_recv.at[side], ctx=partner))
+    sides[0].start()
 
     def down(side, zd):
         sbuf, rbuf = ((sbuf_v, rbuf_v), (sbuf_k, rbuf_k))[side]
@@ -292,14 +256,14 @@
 
     def step(side, zd):
         own, slots, pslots, sbuf, rbuf, out = (
-            (own_v, slot_v, pslot_v, sbuf_v, rbuf_v, gv_ref),
-            (own_k, slot_k, pslot_k, sbuf_k, rbuf_k, gk_ref),
+            (dv_acc, slot_v, pslot_v, sbuf_v, rbuf_v, gv_ref),
+            (dk_acc, slot_k, pslot_k, sbuf_k, rbuf_k, gk_ref),
         )[side]
 
         @pl.when(zd <= z)
         def _():
             dest = 2 * zd + y
-            value = jnp.zeros(own.shape, F32)
+            value = jnp.zeros(own.shape[1:], F32)
             for owner, held in ((c, slots), (partner, pslots)):
                 for j in range(2):
                     gate = jnp.where(picks[owner, j] == dest, 1.0, 0.0).astype(F32)
@@ -317,7 +281,7 @@
 
             @pl.when(zd == z)
             def _():
-                out[...] = (sbuf[zd].astype(F32) + own[...]).astype(BF16)
+                out[...] = (sbuf[zd].astype(F32) + own[0]).astype(BF16)
 
     later = list(range(lines))
 
@@ -327,9 +291,33 @@
                 sides[1].wait()
             step(1, later.pop(0))
 
-    sides[0].wait()
-    for zd in range(lines):
-        step(0, zd)
+    def value_steps():
+        sides[0].wait()
+        for zd in range(lines):
+            step(0, zd)
+
+    def key_pass(h, carry):
+        q, g = q_ref[:, columns(h)], g_ref[:, columns(h)]
+        dws = [lax.dot_general(vsel[j], g, nt, preferred_element_type=F32) for j in range(3)]
+        delta = sum(
+            jnp.sum(lows[h, j].astype(F32) * dws[j], axis=0, keepdims=True) for j in range(3)
+        )
+        dq = jnp.zeros((HEAD, BLOCK), F32)
+        for j in range(3):
+            ds = (lows[h, j].astype(F32) * (dws[j] - delta)).astype(BF16)
+            dk_acc[j] += jnp.dot(ds, q, preferred_element_type=F32)
+            dq = dq + jnp.dot(ktr[j], ds, preferred_element_type=F32)
+        dq_ref[:, columns(h)] = (dq * inv_root).T.astype(BF16)
+        pl.when((h == 1) & (z == lines - 1))(value_steps)
+        return carry
+
+    lax.fori_loop(0, GROUP, key_pass, 0)
+    dk_acc[...] = dk_acc[...] * inv_root
+    for j in range(2):
+        slot_k[j] = dk_acc[j + 1].astype(BF16)
+    sides[1].start()
+    xt[...] = x_ref[...].T
+    pl.when(z != lines - 1)(value_steps)
     gv = gv_ref[...]
     rows = x_ref.shape[1] // (n * nf)
     group = x_ref.shape[1] // n
@@ -389,10 +377,9 @@
             down(1, zd).wait_send()
 
 
-def finish_kernel(gk, gv, gw, gk_out, gv_out, gw_out):
-    gk_out[...] = gk[...]
-    gv_out[...] = gv[...]
-    gw_out[...] = gw[...]
+def finish_kernel(*refs):
+    for at in range(4):
+        refs[4 + at][...] = refs[at][...]
 
 
 def on_device(inputs, queries, key_vectors, w_value, grad_out, block_picks):
@@ -417,46 +404,22 @@
         name="gather_kv",
     )(x, k, w_value)
 
-    me = c[None].astype(jnp.int32)
-    block = (1, BLOCK, HEAD)
-    head = pl.BlockSpec((BLOCK, HEAD), lambda h, me, picks: (0, h))
-    fixed2 = pl.BlockSpec((BLOCK, HEAD), lambda h, me, picks: (0, 0))
-    pair = pl.BlockSpec((2, BLOCK, HEAD), lambda h, me, picks: (0, 0, 0))
-    at = [pl.BlockSpec(block, lambda h, me, picks: (me[0], 0, 0))]
-    for j in range(2):
-        at.append(pl.BlockSpec(block, lambda h, me, picks, j=j: (picks[me[0], j], 0, 0)))
-    dq, own_k, own_v, slot_k, slot_v = pl.pallas_call(
-        attend_kernel,
+    rows = x.shape[1] // (n * nf)
+    line_buf = VM((lines, BLOCK, HEAD), BF16)
+    results = pl.pallas_call(
+        lambda *refs: reduce_kernel(n, nf, *refs),
         out_shape=[
             jax.ShapeDtypeStruct((BLOCK, GROUP * HEAD), BF16),
-            jax.ShapeDtypeStruct((BLOCK, HEAD), F32),
-            jax.ShapeDtypeStruct((BLOCK, HEAD), F32),
-            jax.ShapeDtypeStruct((2, BLOCK, HEAD), BF16),
-            jax.ShapeDtypeStruct((2, BLOCK, HEAD), BF16),
-        ],
-        grid_spec=pltpu.PrefetchScalarGridSpec(
-            num_scalar_prefetch=2,
-            grid=(GROUP,),
-            in_specs=[head, head, fixed2, at[1], at[2], at[0], at[1], at[2]],
-            out_specs=[head, fixed2, fixed2, pair, pair],
-            scratch_shapes=[VM((3, BLOCK, HEAD), F32)] * 2,
-        ),
-        compiler_params=pltpu.CompilerParams(vmem_limit_bytes=40 * 2**20),
-        name="attend",
-    )(me, picks, q, g, k, kall, kall, vall, vall, vall)
-
-    rows = x.shape[1] // (n * nf)
-    line_buf = VM((lines, BLOCK, HEAD), BF16)
-    gk, gv, gw = pl.pallas_call(
-        lambda *refs: reduce_kernel(n, nf, *refs),
-        out_shape=[
             jax.ShapeDtypeStruct((BLOCK, HEAD), BF16),
             jax.ShapeDtypeStruct((BLOCK, HEAD), BF16),
             jax.ShapeDtypeStruct((rows, HEAD), BF16),
         ],
-        in_specs=[smem, hbm] + [vmem] * 4,
-        out_specs=[vmem] * 3,
-        scratch_shapes=[VM((2, BLOCK, HEAD), BF16)] * 2
+        in_specs=[smem] + [vmem] * 5,
+        out_specs=[vmem] * 4,
+        scratch_shapes=[VM((3, BLOCK, HEAD), BF16)] * 2
+        + [VM((3, HEAD, BLOCK), BF16), VM((GROUP, 3, BLOCK, BLOCK), BF16)]
+        + [VM((3, BLOCK, HEAD), F32)] * 2
+        + [VM((2, BLOCK, HEAD), BF16)] * 4
         + [line_buf] * 4
         + [
             VM((nf, n, rows, HEAD), F32),
@@ -464,24 +427,24 @@
             VM((nf, n, rows, HEAD), BF16),
         ]
         + [VM((lines, rows, HEAD), BF16)] * 4
-        + [VM(x.shape, BF16), VM(x.shape[::-1], BF16), dma((1,))]
+        + [VM(x.shape[::-1], BF16)]
         + [
             dma((2,)), dma((2,)), dma((2, lines)), dma((2, lines)), dma((nf,)), dma((nf,)),
             dma((2,)), dma((lines,)), dma((lines,)),
         ],
         compiler_params=pltpu.CompilerParams(
-            collective_id=1, has_side_effects=True, vmem_limit_bytes=32 * 2**20
+            collective_id=1, has_side_effects=True, vmem_limit_bytes=42 * 2**20
         ),
         name="reduce_grads",
-    )(picks, x, own_k, own_v, slot_k, slot_v)
-    gk, gv, gw = pl.pallas_call(
+    )(picks, x, q, g, kall, vall)
+    dq, gk, gv, gw = pl.pallas_call(
         finish_kernel,
-        out_shape=[jax.ShapeDtypeStruct(a.shape, BF16) for a in (gk, gv, gw)],
-        in_specs=[vmem] * 3,
-        out_specs=[vmem] * 3,
-        compiler_params=pltpu.CompilerParams(vmem_limit_bytes=4 * 2**20),
+        out_shape=[jax.ShapeDtypeStruct(a.shape, BF16) for a in results],
+        in_specs=[vmem] * 4,
+        out_specs=[vmem] * 4,
+        compiler_params=pltpu.CompilerParams(vmem_limit_bytes=6 * 2**20),
         name="finish",
-    )(gk, gv, gw)
+    )(*results)
     return dq[None], gk[None], gv[None], gw
 
 

time: 97.5 us -> 88.3 us (0.906)
  Pallas kernels: 93.2 us -> 81.8 us
  local copies, waits for them, and re-layouts: 3.3 us -> 5.43 us
    pallas_call x1 -> x0, Pallas kernels: 19.3 us -> none  [on_device(): pl.pallas_call(attend_kernel, out_shape=[jax.ShapeDtypeStruct((BLOCK, GRO...]
    pallas_call x1, Pallas kernels: 56.1 us -> 63.8 us  [on_device(): pl.pallas_call(lambda *refs: reduce_kernel(n, nf, *refs), out_shape=[jax....]
    unnamed x12 -> x10, local copies, waits for them, and re-layouts: 2.46 us -> 4.53 us
where the time goes in v3:
time: 88.3 us; the launch traced here: 88 us
  Pallas kernels  81.8 us (93%)
  local copies, waits for them, and re-layouts  5.43 us (6%)
    pallas_call x1, Pallas kernels, on_device(): pl.pallas_call(lambda *refs: reduce_kernel(n, nf, *refs), out_shape=[jax....  63.8 us
    pallas_call x1, Pallas kernels, on_device(): pl.pallas_call(lambda *refs: gather_kernel(n, nf, *refs), out_shape=[jax....  17.1 us
    unnamed x10, local copies, waits for them, and re-layouts  4.53 us

profile of v3, /device:TPU:0, one launch (start us, length us, event | category | flops | bytes accessed | tf_op | source)
XLA Modules:
  0.0 88.0 jit_solution(1141345724311955140)
XLA Ops:
  0.6 0.0 copy-start
  0.6 0.9 %copy.10.refs_0_ = s32[8,2]{1,0:T(8,128)S(1)} copy(s32[8,2]{0,1:T(2,128)} %bitcast.13) | data formatting | bytes 128 | tf_op jit(solution)/shard_map/squeeze | solution.py:389
  1.5 17.1 %gather_kv.1 = (bf16[8,512,128]{2,1,0:T(8,128)(2,1)}, bf16[8,512,128]{2,1,0:T(8,128)(2,1)}) custom-call(bf16[512,2048]{1,0:T(8,128)(2,1)} %bitcast.8, bf16[512,128]{1,0:T(8,128)(2,1)} %bitcast.12, bf16[512,128]{1,0:T(8,128)(2,1)} %refs_2_.1), custom_call_target="tpu_custom_call" | custom-call | tf_op jit(solution)/shard_map/gather_kv/pallas_call | solution.py:395
  18.6 0.0 copy-done
  18.6 0.0 copy-start.1
  18.7 1.2 %copy-done.1 = bf16[8,512,128]{2,1,0:T(8,128)(2,1)S(1)} copy-done((bf16[8,512,128]{2,1,0:T(8,128)(2,1)S(1)}, bf16[8,512,128]{2,1,0:T(8,128)(2,1)}, u32[]{:S(2)}) %copy-start.1) | copy-done | bytes 1048600
  19.9 0.0 copy-start.2
  19.9 1.2 %copy-done.2 = bf16[8,512,128]{2,1,0:T(8,128)(2,1)S(1)} copy-done((bf16[8,512,128]{2,1,0:T(8,128)(2,1)S(1)}, bf16[8,512,128]{2,1,0:T(8,128)(2,1)}, u32[]{:S(2)}) %copy-start.2) | copy-done | bytes 1048600
  21.1 0.0 copy-start.3
  21.1 1.0 %copy-done.3 = bf16[1,512,512]{2,1,0:T(8,128)(2,1)S(1)} copy-done((bf16[1,512,512]{2,1,0:T(8,128)(2,1)S(1)}, bf16[1,512,512]{2,1,0:T(8,128)(2,1)}, u32[]{:S(2)}) %copy-start.3) | copy-done | bytes 524312
  22.1 0.0 copy-start.4
  22.1 1.0 %copy-done.4 = bf16[1,512,512]{2,1,0:T(8,128)(2,1)S(1)} copy-done((bf16[1,512,512]{2,1,0:T(8,128)(2,1)S(1)}, bf16[1,512,512]{2,1,0:T(8,128)(2,1)}, u32[]{:S(2)}) %copy-start.4) | copy-done | bytes 524312
  23.2 63.8 %reduce_grads.1 = (bf16[512,512]{1,0:T(8,128)(2,1)S(1)}, bf16[512,128]{1,0:T(8,128)(2,1)S(1)}, bf16[512,128]{1,0:T(8,128)(2,1)S(1)}, bf16[64,128]{1,0:T(8,128)(2,1)S(1)}) custom-call(s32[8,2]{1,0:T(8,128)S(1)} %copy.10.refs_0_, bf16[512,2048]{1,0:T(8,128)(2,1)S(1)} %bitcast.9, bf16[512,512]{1,0:T(8,128)(2,1)S(1)} %bitcast.10, bf16[512,512]{1,0:T(8,128)(2,1)S(1)} %bitcast.11, ...), custom_call_target="tpu_custom_call" | custom-call | tf_op jit(solution)/shard_map/reduce_grads/pallas_call | solution.py:409
  87.0 0.9 %finish.1 = (bf16[512,512]{1,0:T(8,128)(2,1)}, bf16[512,128]{1,0:T(8,128)(2,1)}, bf16[512,128]{1,0:T(8,128)(2,1)}, bf16[64,128]{1,0:T(8,128)(2,1)}) custom-call(bf16[512,512]{1,0:T(8,128)(2,1)S(1)} %get-tuple-element.16.refs_0_, bf16[512,128]{1,0:T(8,128)(2,1)S(1)} %get-tuple-element.17.refs_1_, bf16[512,128]{1,0:T(8,128)(2,1)S(1)} %get-tuple-element.18.refs_2_, ...), custom_call_target="tpu_custom_call" | custom-call | tf_op jit(solution)/shard_map/finish/pallas_call | solution.py:440
Async XLA Ops:
  0.6 18.0 %copy-start = (bf16[1,512,2048]{2,1,0:T(8,128)(2,1)S(1)}, bf16[1,512,2048]{2,1,0:T(8,128)(2,1)}, u32[]{:S(2)}) copy-start(bf16[1,512,2048]{2,1,0:T(8,128)(2,1)} %param.6) | copy-start | bytes 6291460
  18.6 1.2 %copy-start.1 = (bf16[8,512,128]{2,1,0:T(8,128)(2,1)S(1)}, bf16[8,512,128]{2,1,0:T(8,128)(2,1)}, u32[]{:S(2)}) copy-start(bf16[8,512,128]{2,1,0:T(8,128)(2,1)} %get-tuple-element.14.refs_4_) | copy-start | bytes 3145732
  19.9 1.2 %copy-start.2 = (bf16[8,512,128]{2,1,0:T(8,128)(2,1)S(1)}, bf16[8,512,128]{2,1,0:T(8,128)(2,1)}, u32[]{:S(2)}) copy-start(bf16[8,512,128]{2,1,0:T(8,128)(2,1)} %get-tuple-element.15.refs_5_) | copy-start | bytes 3145732
  21.1 1.0 %copy-start.3 = (bf16[1,512,512]{2,1,0:T(8,128)(2,1)S(1)}, bf16[1,512,512]{2,1,0:T(8,128)(2,1)}, u32[]{:S(2)}) copy-start(bf16[1,512,512]{2,1,0:T(8,128)(2,1)} %param.7) | copy-start | bytes 1572868
  22.1 1.0 %copy-start.4 = (bf16[1,512,512]{2,1,0:T(8,128)(2,1)S(1)}, bf16[1,512,512]{2,1,0:T(8,128)(2,1)}, u32[]{:S(2)}) copy-start(bf16[1,512,512]{2,1,0:T(8,128)(2,1)} %param.10) | copy-start | bytes 1572868

commit v4 on v3

--- a/solution.py
+++ b/solution.py
@@ -188,8 +188,8 @@
 
 
 def reduce_kernel(
-    n, nf, picks, x_ref, q_ref, g_ref, kall, vall, dq_ref, gk_ref, gv_ref, gw_ref,
-    ksel, vsel, ktr, lows, dk_acc, dv_acc, slot_k, slot_v,
+    n, nf, picks, x_hbm, q_hbm, g_hbm, k_hbm, v_hbm, dq_ref, gk_ref, gv_ref, gw_ref,
+    x_ref, q_ref, g_ref, kall, vall, load, ksel, vsel, ktr, lows, dk_acc, dv_acc, slot_k, slot_v,
     pslot_k, pslot_v, sbuf_k, sbuf_v, rbuf_k, rbuf_v, acc, wsend, wrecv, ysend_buf, yrecv_buf,
     zsend_buf, zrecv_buf, xt, p_send, p_recv, c_send, c_recv, f_send, f_recv, y_sem, z_send, z_recv,
 ):
@@ -197,10 +197,22 @@
     lines = n // 2
     y, z = c % 2, c // 2
     partner = 2 * z + (1 - y)
+    loads = [
+        pltpu.make_async_copy(source, held, load.at[at])
+        for at, (source, held) in enumerate(
+            ((k_hbm, kall), (v_hbm, vall), (q_hbm, q_ref), (g_hbm, g_ref), (x_hbm, x_ref))
+        )
+    ]
+    for copy in loads:
+        copy.start()
     entered = greet(n, nf)
     inv_root = 1.0 / math.sqrt(HEAD)
     scale = inv_root / math.log(2.0)
     nt = (((1,), (1,)), ((), ()))
+    dk_acc[...] = jnp.zeros_like(dk_acc)
+    dv_acc[...] = jnp.zeros_like(dv_acc)
+    for copy in loads[:4]:
+        copy.wait()
     ksel[0] = kall[c]
     vsel[0] = vall[c]
     for j in range(2):
@@ -209,8 +221,6 @@
     for j in range(3):
         ktr[j] = ksel[j].T
     use = [picks[c, j] != c for j in range(2)]
-    dk_acc[...] = jnp.zeros_like(dk_acc)
-    dv_acc[...] = jnp.zeros_like(dv_acc)
 
     def columns(h):
         return pl.ds(pl.multiple_of(h * HEAD, HEAD), HEAD)
@@ -316,6 +326,7 @@
     for j in range(2):
         slot_k[j] = dk_acc[j + 1].astype(BF16)
     sides[1].start()
+    loads[4].wait()
     xt[...] = x_ref[...].T
     pl.when(z != lines - 1)(value_steps)
     gv = gv_ref[...]
@@ -414,9 +425,11 @@
             jax.ShapeDtypeStruct((BLOCK, HEAD), BF16),
             jax.ShapeDtypeStruct((rows, HEAD), BF16),
         ],
-        in_specs=[smem] + [vmem] * 5,
+        in_specs=[smem] + [hbm] * 5,
         out_specs=[vmem] * 4,
-        scratch_shapes=[VM((3, BLOCK, HEAD), BF16)] * 2
+        scratch_shapes=[VM(a.shape, BF16) for a in (x, q, g, kall, vall)]
+        + [dma((5,))]
+        + [VM((3, BLOCK, HEAD), BF16)] * 2
         + [VM((3, HEAD, BLOCK), BF16), VM((GROUP, 3, BLOCK, BLOCK), BF16)]
         + [VM((3, BLOCK, HEAD), F32)] * 2
         + [VM((2, BLOCK, HEAD), BF16)] * 4
@@ -433,7 +446,7 @@
             dma((2,)), dma((lines,)), dma((lines,)),
         ],
         compiler_params=pltpu.CompilerParams(
-            collective_id=1, has_side_effects=True, vmem_limit_bytes=42 * 2**20
+            collective_id=1, has_side_effects=True, vmem_limit_bytes=58 * 2**20
         ),
         name="reduce_grads",
     )(picks, x, q, g, kall, vall)
@@ -442,7 +455,7 @@
         out_shape=[jax.ShapeDtypeStruct(a.shape, BF16) for a in results],
         in_specs=[vmem] * 4,
         out_specs=[vmem] * 4,
-        compiler_params=pltpu.CompilerParams(vmem_limit_bytes=6 * 2**20),
+        compiler_params=pltpu.CompilerParams(vmem_limit_bytes=60 * 2**20),
         name="finish",
     )(*results)
     return dq[None], gk[None], gv[None], gw

time: 88.3 us -> 88 us (level)
  local copies, waits for them, and re-layouts: 5.43 us -> 1.35 us
  Pallas kernels: 81.8 us -> 85.8 us
    unnamed x10 -> x0, local copies, waits for them, and re-layouts: 4.53 us -> none
    pallas_call x1, Pallas kernels: 63.8 us -> 66.7 us  [on_device(): pl.pallas_call(lambda *refs: reduce_kernel(n, nf, *refs), out_shape=[jax....]
    pallas_call x1, Pallas kernels: 0.93 us -> 2.02 us  [on_device(): pl.pallas_call(finish_kernel, out_shape=[jax.ShapeDtypeStruct(a.shape, BF...]
where the time goes in v4:
time: 88 us; the launch traced here: 87.8 us
  Pallas kernels  85.8 us (98%)
  local copies, waits for them, and re-layouts  1.35 us (2%)
    pallas_call x1, Pallas kernels, on_device(): pl.pallas_call(lambda *refs: reduce_kernel(n, nf, *refs), out_shape=[jax....  66.7 us
    pallas_call x1, Pallas kernels, on_device(): pl.pallas_call(lambda *refs: gather_kernel(n, nf, *refs), out_shape=[jax....  17.1 us
    pallas_call x1, Pallas kernels, on_device(): pl.pallas_call(finish_kernel, out_shape=[jax.ShapeDtypeStruct(a.shape, BF...  2.02 us

profile of v4, /device:TPU:0, one launch (start us, length us, event | category | flops | bytes accessed | tf_op | source)
XLA Modules:
  0.0 87.8 jit_solution(8983689682664355237)
XLA Ops:
  0.6 1.3 %copy.10.refs_0_ = s32[8,2]{1,0:T(8,128)} copy(s32[8,2]{0,1:T(2,128)} %bitcast.13) | data formatting | bytes 128 | tf_op jit(solution)/shard_map/squeeze | solution.py:400
  2.0 17.1 %gather_kv.1 = (bf16[8,512,128]{2,1,0:T(8,128)(2,1)}, bf16[8,512,128]{2,1,0:T(8,128)(2,1)}) custom-call(bf16[512,2048]{1,0:T(8,128)(2,1)} %bitcast.8, bf16[512,128]{1,0:T(8,128)(2,1)} %bitcast.12, bf16[512,128]{1,0:T(8,128)(2,1)} %refs_2_.1), custom_call_target="tpu_custom_call" | custom-call | tf_op jit(solution)/shard_map/gather_kv/pallas_call | solution.py:406
  19.1 66.7 %reduce_grads.1 = (bf16[512,512]{1,0:T(8,128)(2,1)}, bf16[512,128]{1,0:T(8,128)(2,1)}, bf16[512,128]{1,0:T(8,128)(2,1)}, bf16[64,128]{1,0:T(8,128)(2,1)}) custom-call(s32[8,2]{1,0:T(8,128)} %copy.10.refs_0_, bf16[512,2048]{1,0:T(8,128)(2,1)} %bitcast.9, bf16[512,512]{1,0:T(8,128)(2,1)} %bitcast.10, bf16[512,512]{1,0:T(8,128)(2,1)} %bitcast.11, ...), custom_call_target="tpu_custom_call" | custom-call | tf_op jit(solution)/shard_map/reduce_grads/pallas_call | solution.py:420
  85.8 2.0 %finish.1 = (bf16[512,512]{1,0:T(8,128)(2,1)}, bf16[512,128]{1,0:T(8,128)(2,1)}, bf16[512,128]{1,0:T(8,128)(2,1)}, bf16[64,128]{1,0:T(8,128)(2,1)}) custom-call(bf16[512,512]{1,0:T(8,128)(2,1)} %get-tuple-element.16.refs_0_, bf16[512,128]{1,0:T(8,128)(2,1)} %get-tuple-element.17.refs_1_, bf16[512,128]{1,0:T(8,128)(2,1)} %get-tuple-element.18.refs_2_, ...), custom_call_target="tpu_custom_call" | custom-call | tf_op jit(solution)/shard_map/finish/pallas_call | solution.py:453
